TPU v7x, 32 devices: a whole 2x2x4 slice. The times are simulated.
32 devices in a mesh: cuts: 2 (over x), section: 4 (over y, core), dp: 4 (over z).
Axes of the slice: x: 2, y: 2, z: 4, core: 2. Of those that a mesh axis runs over, the one named last changes fastest.
Arguments:
- activations: bfloat16 [2, 4, 1024, 4096], P('cuts', 'section', 'dp'), may hold values from -6 to 6
- upstream_grad: bfloat16 [2, 4, 1024, 4096], P('cuts', 'section', 'dp'), may hold values from -6 to 6
- routes: int32 [2, 4, 1024, 4], P('cuts', 'section', 'dp'), may hold values from 0 to 15, as said below
- router_probs: float32 [2, 4, 1024, 4], P('cuts', 'section', 'dp'), may hold values from 0.2 to 1
- gate_weight: bfloat16 [4, 5376, 4096], P('section', 'dp'), may hold values from -0.09375 to 0.09375
- up_weight: bfloat16 [4, 5376, 4096], P('section', 'dp'), may hold values from -0.09375 to 0.09375
- down_weight: bfloat16 [4, 5376, 4096], P('section', 'dp'), may hold values from -0.078125 to 0.078125
Outputs:
- grad_gate: bfloat16 [4, 5376, 4096], P('section', 'dp')
- grad_up: bfloat16 [4, 5376, 4096], P('section', 'dp')
- grad_down: bfloat16 [4, 5376, 4096], P('section', 'dp')
- prev_grad: bfloat16 [2, 4, 1024, 4096], P('cuts', 'section', 'dp')
Inputs may be any that keep to these rules, and one draw needn't show every extreme that they name: `routes`: each token names 4 different experts. In every aligned block of 256 tokens of one replica and section, from 32 to 64 tokens name expert 0, and in every draw some block has exactly 64.
All inputs are finite; a program needn't handle non-finite values.
Results may differ from a plain program's by a relative error of at most 0.025.
Values may be sent and summed in bfloat16 or wider, within the bound.
A program may use at most 192 MiB of HBM per device.

v0:
```python
import jax
import jax.numpy as jnp
from jax import lax
from jax.sharding import PartitionSpec as P

CAP = 64


def from_behind(block, axis, distance):
    devices = range(lax.axis_size(axis))
    route = [(i - distance, i) for i in devices if i - distance in devices]
    return lax.ppermute(block, axis, route)


def contract_last(left, right):
    return lax.dot_general(
        left, right, (((1,), (1,)), ((), ())), preferred_element_type=jnp.float32
    )


def contract_first(left, right):
    return lax.dot_general(
        left, right, (((0,), (0,)), ((), ())), preferred_element_type=jnp.float32
    )


def per_device(
    activations, upstream_grad, routes, router_probs, gate_weight, up_weight, down_weight
):
    local_acts = activations[0, 0]
    local_grads = upstream_grad[0, 0]
    expert_hits = routes[0, 0] == 0
    router_weight = jnp.sum(jnp.where(expert_hits, router_probs[0, 0], jnp.float32(0.0)), axis=1)
    is_routed = jnp.any(expert_hits, axis=1)
    row_index = jnp.cumsum(is_routed.astype(jnp.int32)) - 1
    wanted = jnp.arange(CAP, dtype=jnp.int32)
    picker = ((row_index[None, :] == wanted[:, None]) & is_routed[None, :]).astype(jnp.bfloat16)
    scaled = (router_weight[:, None] * local_grads.astype(jnp.float32)).astype(jnp.bfloat16)
    packed_acts = jnp.dot(picker, local_acts, preferred_element_type=jnp.float32).astype(
        jnp.bfloat16
    )
    packed_grads = jnp.dot(picker, scaled, preferred_element_type=jnp.float32).astype(jnp.bfloat16)
    rows_acts, rows_grads = (
        lax.all_gather(packed_acts, "dp", axis=0, tiled=True),
        lax.all_gather(packed_grads, "dp", axis=0, tiled=True),
    )
    gate_local = gate_weight[0]
    up_local = up_weight[0]
    down_local = down_weight[0]
    gate_pre = contract_last(rows_acts, gate_local)
    up_pre = contract_last(rows_acts, up_local)
    sig_gate = jax.nn.sigmoid(gate_pre)
    silu_gate = gate_pre * sig_gate
    hidden = (silu_gate * up_pre).astype(jnp.bfloat16)
    hidden_grad = contract_last(rows_grads, down_local)
    gate_grad = (hidden_grad * up_pre * sig_gate * (1.0 + gate_pre * (1.0 - sig_gate))).astype(
        jnp.bfloat16
    )
    up_grad = (hidden_grad * silu_gate).astype(jnp.bfloat16)
    down_part = contract_first(hidden, rows_grads)
    gate_part = contract_first(gate_grad, rows_acts)
    up_part = contract_first(up_grad, rows_acts)
    gate_total, up_total, down_total = (
        lax.psum(gate_part.astype(jnp.bfloat16), "cuts").astype(jnp.float32),
        lax.psum(up_part.astype(jnp.bfloat16), "cuts").astype(jnp.float32),
        lax.psum(down_part.astype(jnp.bfloat16), "cuts").astype(jnp.float32),
    )
    input_rows = lax.psum_scatter(
        (
            jnp.dot(gate_grad, gate_local, preferred_element_type=jnp.float32)
            + jnp.dot(up_grad, up_local, preferred_element_type=jnp.float32)
        ).astype(jnp.bfloat16),
        "dp",
        scatter_dimension=0,
        tiled=True,
    )
    token_grad = contract_first(picker, input_rows).astype(jnp.bfloat16)
    prev_grad = from_behind(token_grad[None, None], "section", -1)
    grad_gate = gate_total.astype(jnp.bfloat16)[None]
    grad_up = up_total.astype(jnp.bfloat16)[None]
    grad_down = down_total.astype(jnp.bfloat16)[None]
    return (grad_gate, grad_up, grad_down, prev_grad)


def solution(mesh):
    placed = (
        P("cuts", "section", "dp", None),
        P("cuts", "section", "dp", None),
        P("cuts", "section", "dp", None),
        P("cuts", "section", "dp", None),
        P("section", "dp", None),
        P("section", "dp", None),
        P("section", "dp", None),
    )
    return jax.shard_map(
        per_device,
        mesh=mesh,
        in_specs=placed,
        out_specs=(
            P("section", "dp", None),
            P("section", "dp", None),
            P("section", "dp", None),
            P("cuts", "section", "dp", None),
        ),
        check_vma=False,
    )
```

profile of v0, /device:TPU:17, one launch (start us, length us, event | category | flops | bytes accessed | tf_op | source)
XLA Modules:
  0.0 930.6 jit_solution(12038015153230166244)
XLA Ops:
  7.2 0.0 all-gather.5.cloned.1.call-start
  7.2 0.9 select_reduce_fusion
  8.1 0.3 reduce-window.9
  8.4 0.1 slice.7
  8.5 0.1 slice_reduce_fusion
  8.7 0.1 add_bitcast_fusion
  8.7 0.1 copy-done
  8.8 1.3 convolution_convert_fusion.4
  10.1 0.0 all-gather.3.cloned.1.call-start
  10.1 3.0 convolution_convert_fusion.5
  13.2 0.0 reduce-scatter.2.cloned.1.call-start
  13.2 42.7 %all-gather.5.cloned.1.call-done = bf16[256,4096]{1,0:T(8,128)(2,1)} async-done(((bf16[64,4096]{1,0:T(8,128)(2,1)}), bf16[256,4096]{1,0:T(8,128)(2,1)}) %all-gather.5.cloned.1.call-update) | async-done | bytes 2097168 | tf_op jit(solution)/shard_map/all_gather | solution.py:44
  55.9 9.1 fusion.5
  65.0 8.7 fusion.9
  73.7 29.1 %all-gather.3.cloned.1.call-done = bf16[256,4096]{1,0:T(8,128)(2,1)} async-done(((bf16[64,4096]{1,0:T(8,128)(2,1)}), bf16[256,4096]{1,0:T(8,128)(2,1)}) %all-gather.3.cloned.1.call-update) | async-done | bytes 2097168 | tf_op jit(solution)/shard_map/all_gather | solution.py:45
  102.7 9.1 multiply_convert_fusion.1
  111.9 6.4 fusion.3
  118.3 4.6 fusion.16
  123.0 0.2 all-reduce.3.cloned.1.call-start
  123.2 5.9 fusion.1
  129.1 5.9 fusion
  135.0 5.9 fusion.2
  140.9 25.5 %reduce-scatter.2.cloned.1.call-done = bf16[64,4096]{1,0:T(8,128)(2,1)} async-done(((bf16[256,4096]{1,0:T(8,128)(2,1)}), bf16[64,4096]{1,0:T(8,128)(2,1)}) %reduce-scatter.2.cloned.1.call-update) | async-done | bytes 524304 | tf_op jit(solution)/shard_map/reduce_scatter | solution.py:68
  166.4 1.8 fusion.19
  168.2 2.5 collective-permute-start
  170.8 25.2 %collective-permute-done = bf16[1,1,256,4096]{3,2,1,0:T(8,128)(2,1)S(1)} collective-permute-done((bf16[1,1,256,4096]{3,2,1,0:T(8,128)(2,1)S(1)}, bf16[1,1,256,4096]{3,2,1,0:T(8,128)(2,1)S(1)}, u32[]{:S(2)}, u32[]{:S(2)}) %collective-permute-start) | collective-permute-done | bytes 2097184 | tf_op jit(solution)/shard_map/ppermute | solution.py:12
  196.0 703.3 %all-reduce.3.cloned.1.call-done = (bf16[1,1344,4096]{2,1,0:T(8,128)(2,1)}, bf16[1,1344,4096]{2,1,0:T(8,128)(2,1)}, bf16[1,1344,4096]{2,1,0:T(8,128)(2,1)}) async-done(((bf16[1,1344,4096]{2,1,0:T(8,128)(2,1)}, bf16[1,1344,4096]{2,1,0:T(8,128)(2,1)}, bf16[1,1344,4096]{2,1,0:T(8,128)(2,1)}), (bf16[1,1344,4096]{2,1,0:T(8,128)(2,1)}, bf16[1,1344,4096]{2,1,0:T(8,128)(2,1)}, ...) | async-done | bytes 33030160 | tf_op jit(solution)/shard_map/psum | solution.py:64
  899.3 12.1 %copy.15 = bf16[1,1344,4096]{2,1,0:T(8,128)(2,1)} copy(bf16[1,1344,4096]{2,1,0:T(8,128)(2,1)} %get-tuple-element.15) | data formatting | bytes 22020096
  911.3 5.4 copy.16
  916.8 0.8 slice-done.5
  917.6 5.2 copy.17
  922.7 1.3 copy.18
  (37 shorter events, 0.2 us)
Async XLA Ops:
  7.2 1.6 copy-start
  7.2 48.7 %all-gather.5.cloned.1.call-start = ((), (), s32[]{:S(2)}) async-start(), calls=%async_computation.2 | async-start | bytes 2621440 | tf_op jit(solution)/shard_map/all_gather | solution.py:44
  10.1 92.6 %all-gather.3.cloned.1.call-start = ((), (), s32[]{:S(2)}) async-start(), calls=%async_computation.1 | async-start | bytes 2621440 | tf_op jit(solution)/shard_map/all_gather | solution.py:45
  13.2 153.3 %reduce-scatter.2.cloned.1.call-start = ((), (), s32[]{:S(2)}) async-start(), calls=%async_computation.3 | async-start | bytes 2621440 | tf_op jit(solution)/shard_map/reduce_scatter | solution.py:68
  55.9 9.1 copy-start.3
  102.7 15.5 %slice-start = ((s8[11010048]{0:T(1024)(128)(4,1)}), s8[4194304]{0:T(1024)(128)(4,1)S(1)}, s32[]{:S(2)}) async-start(s8[11010048]{0:T(1024)(128)(4,1)} %bitcast.51), calls=%async_computation.5 | async-start | bytes 8388608
  102.7 15.5 %slice-start.1 = ((s8[11010048]{0:T(1024)(128)(4,1)}), s8[4194304]{0:T(1024)(128)(4,1)S(1)}, s32[]{:S(2)}) async-start(s8[11010048]{0:T(1024)(128)(4,1)} %bitcast.51), calls=%async_computation.6 | async-start | bytes 8388608
  111.9 6.4 slice-start.2
  123.0 776.3 %all-reduce.3.cloned.1.call-start = ((), (), s32[]{:S(2)}) async-start(), calls=%async_computation.4 | async-start | bytes 66060288 | tf_op jit(solution)/shard_map/psum | solution.py:64
  129.1 5.9 copy-start.6
  129.1 5.9 copy-start.7
  129.1 5.9 copy-start.8
  168.2 27.8 %collective-permute-start = (bf16[1,1,256,4096]{3,2,1,0:T(8,128)(2,1)S(1)}, bf16[1,1,256,4096]{3,2,1,0:T(8,128)(2,1)S(1)}, u32[]{:S(2)}, u32[]{:S(2)}) collective-permute-start(bf16[1,1,256,4096]{3,2,1,0:T(8,128)(2,1)S(1)} %fusion.19), channel_id=1, source_target_pairs={{4,0},{8,4},{12,8},{5,1},{9,5},{13,9},{6,2},{10,6},{14,10},{7,3},{... | collective-permute-start | bytes 6291464 | tf_op jit(solution)/shard_map/ppermute | solution.py:12
  196.0 715.3 %copy-start.4 = (bf16[1,1,256,4096]{3,2,1,0:T(8,128)(2,1)}, bf16[1,1,256,4096]{3,2,1,0:T(8,128)(2,1)S(1)}, u32[]{:S(2)}) copy-start(bf16[1,1,256,4096]{3,2,1,0:T(8,128)(2,1)S(1)} %collective-permute-done) | copy-start | bytes 6291460
  899.3 12.1 %copy-start.2 = (bf16[1,1344,4096]{2,1,0:T(8,128)(2,1)S(1)}, bf16[1,1344,4096]{2,1,0:T(8,128)(2,1)}, u32[]{:S(2)}) copy-start(bf16[1,1344,4096]{2,1,0:T(8,128)(2,1)} %get-tuple-element.16) | copy-start | bytes 33030148
  899.3 17.5 %slice-start.3 = ((s8[11010048]{0:T(1024)(128)(4,1)}), s8[4194304]{0:T(1024)(128)(4,1)S(1)}, s32[]{:S(2)}) async-start(s8[11010048]{0:T(1024)(128)(4,1)} %bitcast.53), calls=%async_computation.8 | async-start | bytes 8388608
  899.3 17.5 %slice-start.4 = ((s8[11010048]{0:T(1024)(128)(4,1)}), s8[4194304]{0:T(1024)(128)(4,1)S(1)}, s32[]{:S(2)}) async-start(s8[11010048]{0:T(1024)(128)(4,1)} %bitcast.53), calls=%async_computation.9 | async-start | bytes 8388608
  911.3 6.2 slice-start.5
  917.6 5.2 copy-start.5
  917.6 6.5 copy-start.1
Sparse Core Ops, SparseCore 0:
  10.2 45.6 all-gather.4
  58.0 44.6 all-gather.2
  123.1 43.3 reduce-scatter.1
  169.8 729.3 all-reduce.2
where the time goes:
time: 933 us; the launch traced here: 931 us
  waiting for transfers between devices  826 us (89%)
  matrix products  61.6 us (7%)
  local copies, waits for them, and re-layouts  25.1 us (3%)
  between operations  13.9 us (1%)
    psum x1, waiting for transfers between devices, per_device(): lax.psum(gate_part.astype(jnp.bfloat16), 'cuts').astype(jnp.float32)  703 us
    all_gather x1, waiting for transfers between devices, per_device(): lax.all_gather(packed_acts, 'dp', axis=0, tiled=True)  42.7 us
    all_gather x1, waiting for transfers between devices, per_device(): lax.all_gather(packed_grads, 'dp', axis=0, tiled=True)  29.1 us
    dot_general x3, matrix products, contract_last(): lax.dot_general(left, right, (((1,), (1,)), ((), ())), preferred_element_...  26.9 us
    reduce_scatter x1, waiting for transfers between devices, per_device(): lax.psum_scatter((jnp.dot(gate_grad, gate_local, preferred_element_type=j...  25.5 us
    ppermute x1, waiting for transfers between devices, from_behind(): return lax.ppermute(block, axis, route)  25.2 us
    unnamed x34, local copies, waits for them, and re-layouts  24.9 us
    dot_general x4, matrix products, contract_first(): lax.dot_general(left, right, (((0,), (0,)), ((), ())), preferred_element_...  19.4 us
  transfers between devices with their start and end apart: 5, of which 5 were waited for; matrix products, arithmetic and copies ran while one was open for 4% of the time, Pallas kernels for 0%

commit v1 on v0

--- a/solution.py
+++ b/solution.py
@@ -24,6 +24,20 @@
     )
 
 
+def hidden_backward(rows_acts, rows_grads, gate_local, up_local, down_local):
+    gate_pre = contract_last(rows_acts, gate_local)
+    up_pre = contract_last(rows_acts, up_local)
+    sig_gate = jax.nn.sigmoid(gate_pre)
+    silu_gate = gate_pre * sig_gate
+    hidden = (silu_gate * up_pre).astype(jnp.bfloat16)
+    hidden_grad = contract_last(rows_grads, down_local)
+    gate_grad = (hidden_grad * up_pre * sig_gate * (1.0 + gate_pre * (1.0 - sig_gate))).astype(
+        jnp.bfloat16
+    )
+    up_grad = (hidden_grad * silu_gate).astype(jnp.bfloat16)
+    return hidden, gate_grad, up_grad
+
+
 def per_device(
     activations, upstream_grad, routes, router_probs, gate_weight, up_weight, down_weight
 ):
@@ -40,30 +54,15 @@
         jnp.bfloat16
     )
     packed_grads = jnp.dot(picker, scaled, preferred_element_type=jnp.float32).astype(jnp.bfloat16)
-    rows_acts, rows_grads = (
-        lax.all_gather(packed_acts, "dp", axis=0, tiled=True),
-        lax.all_gather(packed_grads, "dp", axis=0, tiled=True),
-    )
     gate_local = gate_weight[0]
     up_local = up_weight[0]
     down_local = down_weight[0]
-    gate_pre = contract_last(rows_acts, gate_local)
-    up_pre = contract_last(rows_acts, up_local)
-    sig_gate = jax.nn.sigmoid(gate_pre)
-    silu_gate = gate_pre * sig_gate
-    hidden = (silu_gate * up_pre).astype(jnp.bfloat16)
-    hidden_grad = contract_last(rows_grads, down_local)
-    gate_grad = (hidden_grad * up_pre * sig_gate * (1.0 + gate_pre * (1.0 - sig_gate))).astype(
-        jnp.bfloat16
-    )
-    up_grad = (hidden_grad * silu_gate).astype(jnp.bfloat16)
-    down_part = contract_first(hidden, rows_grads)
-    gate_part = contract_first(gate_grad, rows_acts)
-    up_part = contract_first(up_grad, rows_acts)
-    gate_total, up_total, down_total = (
-        lax.psum(gate_part.astype(jnp.bfloat16), "cuts").astype(jnp.float32),
-        lax.psum(up_part.astype(jnp.bfloat16), "cuts").astype(jnp.float32),
-        lax.psum(down_part.astype(jnp.bfloat16), "cuts").astype(jnp.float32),
+    rows_acts = lax.all_gather(packed_acts, "dp", axis=0, tiled=True)
+    rows_grads = lax.all_gather(packed_grads, "dp", axis=0, tiled=True)
+    both_acts = lax.all_gather(rows_acts, "cuts", axis=0, tiled=True)
+    both_grads = lax.all_gather(rows_grads, "cuts", axis=0, tiled=True)
+    _, gate_grad, up_grad = hidden_backward(
+        rows_acts, rows_grads, gate_local, up_local, down_local
     )
     input_rows = lax.psum_scatter(
         (
@@ -74,11 +73,19 @@
         scatter_dimension=0,
         tiled=True,
     )
-    token_grad = contract_first(picker, input_rows).astype(jnp.bfloat16)
-    prev_grad = from_behind(token_grad[None, None], "section", -1)
-    grad_gate = gate_total.astype(jnp.bfloat16)[None]
-    grad_up = up_total.astype(jnp.bfloat16)[None]
-    grad_down = down_total.astype(jnp.bfloat16)[None]
+    hidden, gate_grad, up_grad = hidden_backward(
+        both_acts, both_grads, gate_local, up_local, down_local
+    )
+    grad_gate = contract_first(gate_grad, both_acts).astype(jnp.bfloat16)[None]
+    grad_up = contract_first(up_grad, both_acts).astype(jnp.bfloat16)[None]
+    grad_down = contract_first(hidden, both_grads).astype(jnp.bfloat16)[None]
+    slot = jnp.where(is_routed, row_index, -1).astype(jnp.bfloat16)
+    behind_rows = from_behind(input_rows, "section", -1)
+    behind_slot = from_behind(slot + 1.0, "section", -1) - 1.0
+    behind_picker = (
+        behind_slot[None, :].astype(jnp.int32) == wanted[:, None]
+    ).astype(jnp.bfloat16)
+    prev_grad = contract_first(behind_picker, behind_rows).astype(jnp.bfloat16)[None, None]
     return (grad_gate, grad_up, grad_down, prev_grad)
 
 

time: 933 us -> 348 us (0.37)
  waiting for transfers between devices: 826 us -> 214 us
  matrix products: 61.6 us -> 111 us
  local copies, waits for them, and re-layouts: 25.1 us -> 0.28 us
    psum x1 -> x0, waiting for transfers between devices: 703 us -> none  [per_device(): lax.psum(gate_part.astype(jnp.bfloat16), 'cuts').astype(jnp.float32)]
    all_gather x2 -> x4, waiting for transfers between devices: 71.7 us -> 174 us  [the longest x1 55.6 us: per_device(): both_acts = lax.all_gather(rows_acts, 'cuts', axis=0, tiled=True)]
    unnamed x34 -> x14, local copies, waits for them, and re-layouts: 24.9 us -> 0.09 us
    ppermute x1 -> x2, waiting for transfers between devices: 25.2 us -> 2.3 us  [from_behind(): return lax.ppermute(block, axis, route)]
    dot_general x3 -> x5, matrix products: 26.9 us -> 46.5 us  [contract_last(): lax.dot_general(left, right, (((1,), (1,)), ((), ())), preferred_element_...]
    dot_general x1, matrix products: 6.36 us -> 22 us  [per_device(): jnp.dot(gate_grad, gate_local, preferred_element_type=jnp.float32)]
    reduce_scatter x1, waiting for transfers between devices: 25.5 us -> 37.4 us  [per_device(): lax.psum_scatter((jnp.dot(gate_grad, gate_local, preferred_element_type=j...]
  transfers between devices with their start and end apart: 5 -> 7, of which waited for: 5 -> 6; matrix products, arithmetic and copies ran while one was open for 4% -> 20% of each run, Pallas kernels for 0% -> 0%
where the time goes in v1:
time: 348 us; the launch traced here: 346 us
  waiting for transfers between devices  214 us (61%)
  matrix products  111 us (32%)
  between operations  13.9 us (4%)
  starting transfers between devices  5.3 us (2%)
    all_gather x1, waiting for transfers between devices, per_device(): both_acts = lax.all_gather(rows_acts, 'cuts', axis=0, tiled=True)  55.6 us
    dot_general x5, matrix products, contract_last(): lax.dot_general(left, right, (((1,), (1,)), ((), ())), preferred_element_...  46.5 us
    all_gather x1, waiting for transfers between devices, per_device(): rows_acts = lax.all_gather(packed_acts, 'dp', axis=0, tiled=True)  42.7 us
    all_gather x1, waiting for transfers between devices, per_device(): rows_grads = lax.all_gather(packed_grads, 'dp', axis=0, tiled=True)  40.3 us
    reduce_scatter x1, waiting for transfers between devices, per_device(): lax.psum_scatter((jnp.dot(gate_grad, gate_local, preferred_element_type=j...  37.4 us
    all_gather x1, waiting for transfers between devices, per_device(): both_grads = lax.all_gather(rows_grads, 'cuts', axis=0, tiled=True)  35 us
    dot_general x4, matrix products, contract_first(): lax.dot_general(left, right, (((0,), (0,)), ((), ())), preferred_element_...  28.6 us
    dot_general x1, matrix products, per_device(): jnp.dot(gate_grad, gate_local, preferred_element_type=jnp.float32)  22 us
  transfers between devices with their start and end apart: 7, of which 6 were waited for; matrix products, arithmetic and copies ran while one was open for 20% of the time, Pallas kernels for 0%

profile of v1, /device:TPU:17, one launch (start us, length us, event | category | flops | bytes accessed | tf_op | source)
XLA Modules:
  0.0 346.2 jit_solution(6932482612302510799)
XLA Ops:
  7.2 0.9 select_reduce_fusion
  8.1 0.3 reduce-window.9
  8.4 0.1 slice.7
  8.5 0.1 slice_reduce_fusion
  8.7 0.1 fusion.59
  8.7 0.1 copy-done
  8.8 1.3 convolution_convert_fusion.4
  10.1 0.0 all-gather.5.cloned.1.call-start
  10.1 3.0 convolution_convert_fusion.5
  13.2 0.0 reduce-scatter.2.cloned.1.call-start
  13.2 42.7 %all-gather.9.cloned.1.call-done = bf16[256,4096]{1,0:T(8,128)(2,1)} async-done(((bf16[64,4096]{1,0:T(8,128)(2,1)}), bf16[256,4096]{1,0:T(8,128)(2,1)}) %all-gather.9.cloned.1.call-update) | async-done | bytes 2097168 | tf_op jit(solution)/shard_map/all_gather | solution.py:60
  55.9 6.5 %fusion.5 = f32[256,1344]{0,1:T(8,128)S(1)} fusion(bf16[256,4096]{1,0:T(8,128)(2,1)} %all-gather.9.cloned.1.call-done, bf16[1,1344,4096]{2,1,0:T(8,128)(2,1)} %param.11), kind=kOutput, calls=%fused_computation.8 | convolution fusion | flops 2818572288 | bytes 14483456 | tf_op jit(solution)/shard_map/dot_general | solution.py:16
  62.4 40.3 %all-gather.5.cloned.1.call-done = bf16[256,4096]{1,0:T(8,128)(2,1)} async-done(((bf16[64,4096]{1,0:T(8,128)(2,1)}), bf16[256,4096]{1,0:T(8,128)(2,1)}) %all-gather.5.cloned.1.call-update) | async-done | bytes 2097168 | tf_op jit(solution)/shard_map/all_gather | solution.py:61
  102.7 6.7 %fusion.15 = f32[256,1344]{0,1:T(8,128)S(1)} fusion(bf16[256,4096]{1,0:T(8,128)(2,1)} %all-gather.5.cloned.1.call-done, bf16[1,1344,4096]{2,1,0:T(8,128)(2,1)} %param.13), kind=kOutput, calls=%fused_computation.18 | convolution fusion | flops 2818572288 | bytes 14483456 | tf_op jit(solution)/shard_map/dot_general | solution.py:16
  109.4 22.0 %fusion.3 = f32[256,4096]{1,0:T(8,128)} fusion(bf16[1,1344,4096]{2,1,0:T(8,128)(2,1)} %param.11, f32[256,1344]{0,1:T(8,128)S(1)} %fusion.15, bf16[256,4096]{1,0:T(8,128)(2,1)} %all-gather.9.cloned.1.call-done, bf16[1,1344,4096]{2,1,0:T(8,128)(2,1)} %param.12, f32[256,1344]{0,1:T(8,128)S(1)} %fusion.5), kind=kOutput, calls=%fused_computation.6 | convolution fusion | flops 5640585216 | bytes 31064064 | tf_op jit(solution)/shard_map/dot_general | solution.py:69
  131.5 9.6 %fusion.22 = bf16[256,4096]{1,0:T(8,128)(2,1)} fusion(f32[256,4096]{1,0:T(8,128)} %fusion.3, bf16[1,1344,4096]{2,1,0:T(8,128)(2,1)} %param.12, f32[256,1344]{0,1:T(8,128)S(1)} %fusion.15, f32[256,1344]{0,1:T(8,128)S(1)} %fusion.5), kind=kOutput, calls=%fused_computation.23 | convolution fusion | flops 2822733824 | bytes 20054016 | tf_op jit(solution)/shard_map/dot_general | solution.py:70
  141.0 0.0 all-gather.11.cloned.1.call-start
  141.1 0.5 all-gather.11.cloned.1.call-update
  141.7 0.5 all-gather.7.cloned.1.call-update
  142.2 2.6 collective-permute-start
  144.8 2.3 collective-permute-done
  147.1 37.4 %reduce-scatter.2.cloned.1.call-done = bf16[64,4096]{1,0:T(8,128)(2,1)} async-done(((bf16[256,4096]{1,0:T(8,128)(2,1)}), bf16[64,4096]{1,0:T(8,128)(2,1)}) %reduce-scatter.2.cloned.1.call-update) | async-done | bytes 524304 | tf_op jit(solution)/shard_map/reduce_scatter | solution.py:67
  184.5 2.5 collective-permute-start.1
  187.0 55.6 %all-gather.11.cloned.1.call-done = bf16[512,4096]{1,0:T(8,128)(2,1)} async-done(((bf16[256,4096]{1,0:T(8,128)(2,1)}), bf16[512,4096]{1,0:T(8,128)(2,1)}) %all-gather.11.cloned.1.call-update) | async-done | bytes 4194320 | tf_op jit(solution)/shard_map/all_gather | solution.py:62
  242.7 12.3 %fusion.7 = f32[512,1344]{0,1:T(8,128)} fusion(bf16[512,4096]{1,0:T(8,128)(2,1)} %all-gather.11.cloned.1.call-done, bf16[1,1344,4096]{2,1,0:T(8,128)(2,1)} %param.11), kind=kOutput, calls=%fused_computation.10 | convolution fusion | flops 5637144576 | bytes 17956864 | tf_op jit(solution)/shard_map/dot_general | solution.py:16
  255.0 11.0 %fusion.13 = f32[512,1344]{0,1:T(8,128)} fusion(bf16[512,4096]{1,0:T(8,128)(2,1)S(1)} %copy-done.2, bf16[1,1344,4096]{2,1,0:T(8,128)(2,1)} %param.12), kind=kOutput, calls=%fused_computation.16 | convolution fusion | flops 5637144576 | bytes 17956864 | tf_op jit(solution)/shard_map/dot_general | solution.py:16
  265.9 35.0 %all-gather.7.cloned.1.call-done = bf16[512,4096]{1,0:T(8,128)(2,1)} async-done(((bf16[256,4096]{1,0:T(8,128)(2,1)}), bf16[512,4096]{1,0:T(8,128)(2,1)}) %all-gather.7.cloned.1.call-update) | async-done | bytes 4194320 | tf_op jit(solution)/shard_map/all_gather | solution.py:63
  300.9 10.1 %fusion.17 = f32[512,1344]{0,1:T(8,128)S(1)} fusion(bf16[512,4096]{1,0:T(8,128)(2,1)} %all-gather.7.cloned.1.call-done, bf16[1,1344,4096]{2,1,0:T(8,128)(2,1)} %param.13), kind=kOutput, calls=%fused_computation.20 | convolution fusion | flops 5637144576 | bytes 17956864 | tf_op jit(solution)/shard_map/dot_general | solution.py:16
  311.0 8.6 %fusion.2 = bf16[1,1344,4096]{2,1,0:T(8,128)(2,1)} fusion(bf16[512,4096]{1,0:T(8,128)(2,1)S(1)} %copy-done.4, f32[512,1344]{0,1:T(8,128)S(1)} %copy-done.6, f32[512,1344]{0,1:T(8,128)S(1)} %copy-done.5), kind=kOutput, calls=%fused_computation.5 | convolution fusion | flops 5646778368 | bytes 20709376 | tf_op jit(solution)/shard_map/dot_general | solution.py:22
  319.7 9.3 %fusion = bf16[1,1344,4096]{2,1,0:T(8,128)(2,1)} fusion(bf16[512,4096]{1,0:T(8,128)(2,1)S(1)} %copy-done.3, f32[512,1344]{0,1:T(8,128)S(1)} %copy-done.5, f32[512,1344]{0,1:T(8,128)S(1)} %fusion.17, f32[512,1344]{0,1:T(8,128)S(1)} %copy-done.6), kind=kOutput, calls=%fused_computation.3 | convolution fusion | flops 5649530880 | bytes 23461888 | tf_op jit(solution)/shard_map/dot_general | solution.py:22
  329.0 8.6 %fusion.1 = bf16[1,1344,4096]{2,1,0:T(8,128)(2,1)} fusion(bf16[512,4096]{1,0:T(8,128)(2,1)S(1)} %copy-done.3, f32[512,1344]{0,1:T(8,128)S(1)} %fusion.17, f32[512,1344]{0,1:T(8,128)S(1)} %copy-done.5), kind=kOutput, calls=%fused_computation.4 | convolution fusion | flops 5646778368 | bytes 20709376 | tf_op jit(solution)/shard_map/dot_general | solution.py:22
  337.6 2.1 fusion.25
  (23 shorter events, 0.2 us)
Async XLA Ops:
  7.2 1.6 copy-start
  7.2 48.7 %all-gather.9.cloned.1.call-start = ((), (), s32[]{:S(2)}) async-start(), calls=%async_computation.3 | async-start | bytes 2621440 | tf_op jit(solution)/shard_map/all_gather | solution.py:60
  10.1 92.6 %all-gather.5.cloned.1.call-start = ((), (), s32[]{:S(2)}) async-start(), calls=%async_computation.1 | async-start | bytes 2621440 | tf_op jit(solution)/shard_map/all_gather | solution.py:61
  13.2 171.3 %reduce-scatter.2.cloned.1.call-start = ((), (), s32[]{:S(2)}) async-start(), calls=%async_computation.5 | async-start | bytes 2621440 | tf_op jit(solution)/shard_map/reduce_scatter | solution.py:67
  141.0 101.7 %all-gather.11.cloned.1.call-start = ((), (), s32[]{:S(2)}) async-start(), calls=%async_computation.4 | async-start | bytes 6291456 | tf_op jit(solution)/shard_map/all_gather | solution.py:62
  141.6 159.3 %all-gather.7.cloned.1.call-start = ((), (), s32[]{:S(2)}) async-start(), calls=%async_computation.2 | async-start | bytes 6291456 | tf_op jit(solution)/shard_map/all_gather | solution.py:63
  142.2 4.9 %collective-permute-start = (bf16[256]{0:T(256)(128)(2,1)S(1)}, bf16[256]{0:T(256)(128)(2,1)S(1)}, u32[]{:S(2)}, u32[]{:S(2)}) collective-permute-start(bf16[256]{0:T(256)(128)(2,1)S(1)} %get-tuple-element.4), channel_id=1, source_target_pairs={{4,0},{8,4},{12,8},{5,1},{9,5},{13,9},{6,2},{10,6},{14,10},{7,3},{... | collective-permute-start | bytes 1544 | tf_op jit(solution)/shard_map/ppermute | solution.py:12
  184.5 153.1 %collective-permute-start.1 = (bf16[64,4096]{1,0:T(8,128)(2,1)}, bf16[64,4096]{1,0:T(8,128)(2,1)S(1)}, u32[]{:S(2)}, u32[]{:S(2)}) collective-permute-start(bf16[64,4096]{1,0:T(8,128)(2,1)} %reduce-scatter.2.cloned.1.call-done), channel_id=1, source_target_pairs={{4,0},{8,4},{12,8},{5,1},{9,5},{13,9},{6,2},{10,6},{14,10},{7,3},{... | collective-permute-start | bytes 1572872 | tf_op jit(solution)/shard_map/ppermute | solution.py:12
  242.7 12.3 %copy-start.2 = (bf16[512,4096]{1,0:T(8,128)(2,1)S(1)}, bf16[512,4096]{1,0:T(8,128)(2,1)}, u32[]{:S(2)}) copy-start(bf16[512,4096]{1,0:T(8,128)(2,1)} %all-gather.11.cloned.1.call-done) | copy-start | bytes 12582916
  300.9 10.1 %copy-start.4 = (bf16[512,4096]{1,0:T(8,128)(2,1)S(1)}, bf16[512,4096]{1,0:T(8,128)(2,1)}, u32[]{:S(2)}) copy-start(bf16[512,4096]{1,0:T(8,128)(2,1)} %all-gather.7.cloned.1.call-done) | copy-start | bytes 12582916
  300.9 10.1 %copy-start.5 = (f32[512,1344]{0,1:T(8,128)S(1)}, f32[512,1344]{0,1:T(8,128)}, u32[]{:S(2)}) copy-start(f32[512,1344]{0,1:T(8,128)} %fusion.7) | copy-start | bytes 8257540
  300.9 10.1 %copy-start.6 = (f32[512,1344]{0,1:T(8,128)S(1)}, f32[512,1344]{0,1:T(8,128)}, u32[]{:S(2)}) copy-start(f32[512,1344]{0,1:T(8,128)} %fusion.13) | copy-start | bytes 8257540
  311.0 8.6 %copy-start.3 = (bf16[512,4096]{1,0:T(8,128)(2,1)S(1)}, bf16[512,4096]{1,0:T(8,128)(2,1)}, u32[]{:S(2)}) copy-start(bf16[512,4096]{1,0:T(8,128)(2,1)} %all-gather.11.cloned.1.call-done) | copy-start | bytes 12582916
  329.0 10.7 %copy-start.1 = (bf16[1,1,256,4096]{3,2,1,0:T(8,128)(2,1)S(1)}, bf16[1,1,256,4096]{3,2,1,0:T(8,128)(2,1)}, u32[]{:S(2)}) copy-start(bf16[1,1,256,4096]{3,2,1,0:T(8,128)(2,1)} %param.7) | copy-start | bytes 6291460
Sparse Core Ops, SparseCore 0:
  10.2 45.6 all-gather.8
  58.0 44.6 all-gather.4
  141.2 43.3 reduce-scatter.1
  186.0 56.6 all-gather.10
  244.1 56.7 all-gather.6

commit v2 on v1

--- a/solution.py
+++ b/solution.py
@@ -1,6 +1,10 @@
+import functools
+
 import jax
 import jax.numpy as jnp
 from jax import lax
+from jax.experimental import pallas as pl
+from jax.experimental.pallas import tpu as pltpu
 from jax.sharding import PartitionSpec as P
 
 CAP = 64
@@ -36,6 +40,296 @@
     )
     up_grad = (hidden_grad * silu_gate).astype(jnp.bfloat16)
     return hidden, gate_grad, up_grad
+
+
+TILES = 3
+VMEM_BUDGET = 60 * 2**20
+
+
+def exchange_kernel(
+    n, acts_in, grads_in, gate_hbm, up_hbm, down_hbm,
+    acts_out, grads_out, hidden_o, gate_o, up_o, input_o,
+    acts_buf, grads_buf, gate_w, up_w, down_w, gate_t, up_t, part, from_low, from_high,
+    own_sem, weight_sem, out_sem, z_recv, up_send, down_send, x_recv, x_send,
+    low_recv, high_recv, sum_up_send, sum_down_send,
+):
+    i = lax.axis_index("dp")
+    c = lax.axis_index("cuts")
+    other = 1 - c
+    cap = acts_in.shape[0]
+    rows = n * cap
+    hid, width = gate_w.shape
+    tile = hid // TILES
+    bufs = (acts_buf, grads_buf)
+    has_low, has_high = i > 0, i < n - 1
+    low, high, across = {"dp": i - 1}, {"dp": i + 1}, {"cuts": other}
+
+    weight_copies = [
+        pltpu.make_async_copy(src, dst, weight_sem.at[k])
+        for k, (src, dst) in enumerate(
+            ((gate_hbm, gate_w), (up_hbm, up_w), (down_hbm, down_w))
+        )
+    ]
+
+    def slot(kind, replica, j):
+        return bufs[kind].at[replica, pl.ds(pl.multiple_of(j * cap, cap), cap), :]
+
+    own_copies = [
+        pltpu.make_async_copy(src, slot(kind, c, i), own_sem.at[kind])
+        for kind, src in enumerate((acts_in, grads_in))
+    ]
+    for copy in own_copies:
+        copy.start()
+
+    barrier = pltpu.get_barrier_semaphore()
+
+    def greet(where):
+        pl.semaphore_signal(
+            barrier, inc=1, device_id=where, device_id_type=pl.DeviceIdType.MESH
+        )
+
+    pl.when(has_low)(lambda: greet(low))
+    pl.when(has_high)(lambda: greet(high))
+    greet(across)
+    pl.semaphore_wait(barrier, 1 + jnp.int32(has_low) + jnp.int32(has_high))
+    for copy in own_copies:
+        copy.wait()
+
+    def send(kind, j, where, send_sem, recv_sem):
+        return pltpu.make_async_remote_copy(
+            src_ref=slot(kind, c, j),
+            dst_ref=slot(kind, c, j),
+            send_sem=send_sem.at[kind, j],
+            recv_sem=recv_sem.at[kind, j],
+            device_id=where,
+            device_id_type=pl.DeviceIdType.MESH,
+        )
+
+    def to_high(kind, j):
+        return send(kind, j, high, up_send, z_recv)
+
+    def to_low(kind, j):
+        return send(kind, j, low, down_send, z_recv)
+
+    def to_other(kind, j):
+        return send(kind, j, across, x_send, x_recv)
+
+    def from_other(kind, j):
+        return pltpu.make_async_remote_copy(
+            src_ref=slot(kind, other, j),
+            dst_ref=slot(kind, other, j),
+            send_sem=x_send.at[kind, j],
+            recv_sem=x_recv.at[kind, j],
+            device_id=across,
+            device_id_type=pl.DeviceIdType.MESH,
+        )
+
+    for kind in range(2):
+        pl.when(has_high)(lambda kind=kind: to_high(kind, i).start())
+        pl.when(has_low)(lambda kind=kind: to_low(kind, i).start())
+        to_other(kind, i).start()
+    for copy in weight_copies:
+        copy.start()
+    for d in range(1, n):
+        for kind in range(2):
+
+            @pl.when(i - d >= 0)
+            def _(kind=kind, d=d):
+                to_high(kind, i - d).wait_recv()
+                pl.when(has_high)(lambda: to_high(kind, i - d).start())
+                to_other(kind, i - d).start()
+
+            @pl.when(i + d < n)
+            def _(kind=kind, d=d):
+                to_low(kind, i + d).wait_recv()
+                pl.when(has_low)(lambda: to_low(kind, i + d).start())
+                to_other(kind, i + d).start()
+
+    for copy in weight_copies:
+        copy.wait()
+
+    def forward(replica, t):
+        some = pl.ds(pl.multiple_of(t * tile, tile), tile)
+        cols = pl.ds(pl.multiple_of(replica * rows, rows), rows)
+        acts = acts_buf[replica]
+        gate_pre = contract_last(gate_w[some, :], acts)
+        up_pre = contract_last(up_w[some, :], acts)
+        hidden_grad = contract_last(down_w[some, :], grads_buf[replica])
+        sig = jax.nn.sigmoid(gate_pre)
+        silu = gate_pre * sig
+        hidden_o[some, cols] = (silu * up_pre).astype(jnp.bfloat16)
+        gate_o[some, cols] = (
+            hidden_grad * up_pre * sig * (1.0 + gate_pre * (1.0 - sig))
+        ).astype(jnp.bfloat16)
+        up_o[some, cols] = (hidden_grad * silu).astype(jnp.bfloat16)
+
+    @pl.loop(0, TILES)
+    def _(t):
+        forward(c, t)
+
+    own_cols = pl.ds(pl.multiple_of(c * rows, rows), rows)
+    gate_t[...] = jnp.transpose(gate_o[:, own_cols])
+    up_t[...] = jnp.transpose(up_o[:, own_cols])
+    step = 512
+
+    @pl.loop(0, width // step)
+    def _(t):
+        some = pl.ds(pl.multiple_of(t * step, step), step)
+        part[:, some] = (
+            jnp.dot(gate_t[...], gate_w[:, some], preferred_element_type=jnp.float32)
+            + jnp.dot(up_t[...], up_w[:, some], preferred_element_type=jnp.float32)
+        ).astype(jnp.bfloat16)
+
+    def share(j):
+        return pl.ds(pl.multiple_of(j * cap, cap), cap)
+
+    def sum_high(j):
+        return pltpu.make_async_remote_copy(
+            src_ref=part.at[share(j), :],
+            dst_ref=from_low.at[j],
+            send_sem=sum_up_send.at[j],
+            recv_sem=low_recv.at[j],
+            device_id=high,
+            device_id_type=pl.DeviceIdType.MESH,
+        )
+
+    def sum_low(j):
+        return pltpu.make_async_remote_copy(
+            src_ref=part.at[share(j), :],
+            dst_ref=from_high.at[j],
+            send_sem=sum_down_send.at[j],
+            recv_sem=high_recv.at[j],
+            device_id=low,
+            device_id_type=pl.DeviceIdType.MESH,
+        )
+
+    def add_to_part(arrived, j):
+        part[share(j), :] = (
+            part[share(j), :].astype(jnp.float32) + arrived[j].astype(jnp.float32)
+        ).astype(jnp.bfloat16)
+
+    def pass_up(j):
+        @pl.when(i < j)
+        def _():
+            @pl.when(has_low)
+            def _():
+                sum_high(j).wait_recv()
+                add_to_part(from_low, j)
+
+            sum_high(j).start()
+
+    def pass_down(j):
+        @pl.when(i > j)
+        def _():
+            @pl.when(has_high)
+            def _():
+                sum_low(j).wait_recv()
+                add_to_part(from_high, j)
+
+            sum_low(j).start()
+
+    lower_half = 2 * i < n
+    for k in range(n - 1):
+
+        @pl.when(lower_half)
+        def _(k=k):
+            pass_up(n - 1 - k)
+            pass_down(k)
+
+        @pl.when(jnp.logical_not(lower_half))
+        def _(k=k):
+            pass_down(k)
+            pass_up(n - 1 - k)
+
+        if k == 0:
+            for j in range(n):
+                for kind in range(2):
+                    from_other(kind, j).wait_recv()
+            out_copies = [
+                pltpu.make_async_copy(acts_buf, acts_out, out_sem.at[0]),
+                pltpu.make_async_copy(grads_buf, grads_out, out_sem.at[1]),
+            ]
+            for copy in out_copies:
+                copy.start()
+        if k < TILES:
+            forward(other, k)
+    for k in range(n - 1, TILES):
+        forward(other, k)
+
+    total = part[share(i), :].astype(jnp.float32)
+    input_o[...] = total
+
+    @pl.when(has_low)
+    def _():
+        sum_high(i).wait_recv()
+        input_o[...] += from_low[i].astype(jnp.float32)
+
+    @pl.when(has_high)
+    def _():
+        sum_low(i).wait_recv()
+        input_o[...] += from_high[i].astype(jnp.float32)
+
+    for j in range(n):
+        pl.when(i < j)(lambda j=j: sum_high(j).wait_send())
+        pl.when(i > j)(lambda j=j: sum_low(j).wait_send())
+        for kind in range(2):
+            to_other(kind, j).wait_send()
+            pl.when(jnp.logical_and(has_high, i >= j))(
+                lambda kind=kind, j=j: to_high(kind, j).wait_send()
+            )
+            pl.when(jnp.logical_and(has_low, i <= j))(
+                lambda kind=kind, j=j: to_low(kind, j).wait_send()
+            )
+    for copy in out_copies:
+        copy.wait()
+
+
+def kernel_bytes(n, cap, hid, width):
+    weights = 3 * hid * width * 2
+    rows = 4 * n * cap * width * 2
+    hidden = (6 + 2) * hid * n * cap * 2
+    sums = 3 * n * cap * width * 2 + cap * width * 4
+    return weights + rows + hidden + sums
+
+
+def exchange(n, acts, grads, gate_local, up_local, down_local):
+    cap, width = acts.shape
+    hid = gate_local.shape[0]
+    rows = n * cap
+    bf16 = jnp.bfloat16
+    both = jax.ShapeDtypeStruct((2, rows, width), bf16)
+    units = jax.ShapeDtypeStruct((hid, 2 * rows), bf16)
+    anywhere = pl.BlockSpec(memory_space=pl.ANY)
+    vmem = pl.BlockSpec(memory_space=pltpu.VMEM)
+    dma = pltpu.SemaphoreType.DMA
+    return pl.pallas_call(
+        functools.partial(exchange_kernel, n),
+        out_shape=[both, both, units, units, units,
+                   jax.ShapeDtypeStruct((cap, width), jnp.float32)],
+        in_specs=[anywhere] * 5,
+        out_specs=[anywhere, anywhere, vmem, vmem, vmem, vmem],
+        scratch_shapes=[
+            pltpu.VMEM((2, rows, width), bf16),
+            pltpu.VMEM((2, rows, width), bf16),
+            pltpu.VMEM((hid, width), bf16),
+            pltpu.VMEM((hid, width), bf16),
+            pltpu.VMEM((hid, width), bf16),
+            pltpu.VMEM((rows, hid), bf16),
+            pltpu.VMEM((rows, hid), bf16),
+            pltpu.VMEM((rows, width), bf16),
+            pltpu.VMEM((n, cap, width), bf16),
+            pltpu.VMEM((n, cap, width), bf16),
+            dma((2,)), dma((3,)), dma((2,)),
+            dma((2, n)), dma((2, n)), dma((2, n)), dma((2, n)), dma((2, n)),
+            dma((n,)), dma((n,)), dma((n,)), dma((n,)),
+        ],
+        compiler_params=pltpu.CompilerParams(
+            collective_id=0, has_side_effects=True, vmem_limit_bytes=VMEM_BUDGET
+        ),
+        cost_estimate=pl.CostEstimate(
+            flops=16 * rows * hid * width, bytes_accessed=8 * hid * width, transcendentals=0
+        ),
+    )(acts, grads, gate_local, up_local, down_local)
 
 
 def per_device(
@@ -57,28 +351,40 @@
     gate_local = gate_weight[0]
     up_local = up_weight[0]
     down_local = down_weight[0]
-    rows_acts = lax.all_gather(packed_acts, "dp", axis=0, tiled=True)
-    rows_grads = lax.all_gather(packed_grads, "dp", axis=0, tiled=True)
-    both_acts = lax.all_gather(rows_acts, "cuts", axis=0, tiled=True)
-    both_grads = lax.all_gather(rows_grads, "cuts", axis=0, tiled=True)
-    _, gate_grad, up_grad = hidden_backward(
-        rows_acts, rows_grads, gate_local, up_local, down_local
-    )
-    input_rows = lax.psum_scatter(
-        (
-            jnp.dot(gate_grad, gate_local, preferred_element_type=jnp.float32)
-            + jnp.dot(up_grad, up_local, preferred_element_type=jnp.float32)
-        ).astype(jnp.bfloat16),
-        "dp",
-        scatter_dimension=0,
-        tiled=True,
-    )
-    hidden, gate_grad, up_grad = hidden_backward(
-        both_acts, both_grads, gate_local, up_local, down_local
-    )
-    grad_gate = contract_first(gate_grad, both_acts).astype(jnp.bfloat16)[None]
-    grad_up = contract_first(up_grad, both_acts).astype(jnp.bfloat16)[None]
-    grad_down = contract_first(hidden, both_grads).astype(jnp.bfloat16)[None]
+    n = lax.axis_size("dp")
+    hid, width = gate_local.shape
+    if kernel_bytes(n, CAP, hid, width) <= VMEM_BUDGET and hid % (16 * TILES) == 0:
+        acts, grads, hidden, gate_grad, up_grad, input_rows = exchange(
+            n, packed_acts, packed_grads, gate_local, up_local, down_local
+        )
+        input_rows = input_rows.astype(jnp.bfloat16)
+        both_acts = acts.reshape(2 * n * CAP, width)
+        both_grads = grads.reshape(2 * n * CAP, width)
+        summed = functools.partial(jnp.dot, preferred_element_type=jnp.float32)
+    else:
+        rows_acts = lax.all_gather(packed_acts, "dp", axis=0, tiled=True)
+        rows_grads = lax.all_gather(packed_grads, "dp", axis=0, tiled=True)
+        both_acts = lax.all_gather(rows_acts, "cuts", axis=0, tiled=True)
+        both_grads = lax.all_gather(rows_grads, "cuts", axis=0, tiled=True)
+        _, gate_grad, up_grad = hidden_backward(
+            rows_acts, rows_grads, gate_local, up_local, down_local
+        )
+        input_rows = lax.psum_scatter(
+            (
+                jnp.dot(gate_grad, gate_local, preferred_element_type=jnp.float32)
+                + jnp.dot(up_grad, up_local, preferred_element_type=jnp.float32)
+            ).astype(jnp.bfloat16),
+            "dp",
+            scatter_dimension=0,
+            tiled=True,
+        )
+        hidden, gate_grad, up_grad = hidden_backward(
+            both_acts, both_grads, gate_local, up_local, down_local
+        )
+        summed = contract_first
+    grad_gate = summed(gate_grad, both_acts).astype(jnp.bfloat16)[None]
+    grad_up = summed(up_grad, both_acts).astype(jnp.bfloat16)[None]
+    grad_down = summed(hidden, both_grads).astype(jnp.bfloat16)[None]
     slot = jnp.where(is_routed, row_index, -1).astype(jnp.bfloat16)
     behind_rows = from_behind(input_rows, "section", -1)
     behind_slot = from_behind(slot + 1.0, "section", -1) - 1.0

time: 348 us -> 170 us (0.49)
  waiting for transfers between devices: 214 us -> 0.01 us
  Pallas kernels: 0 us -> 124 us
  matrix products: 111 us -> 34.5 us
  between operations: 13.9 us -> 0.71 us
    all_gather x4 -> x0, waiting for transfers between devices: 174 us -> none  [the longest x1 55.6 us: per_device(): both_acts = lax.all_gather(rows_acts, 'cuts', axis=0, tiled=True)]
    pallas_call x0 -> x1, Pallas kernels: none -> 124 us  [exchange(): pl.pallas_call(functools.partial(exchange_kernel, n), out_shape=[both, bo...]
    dot_general x7 -> x3, matrix products: 78.1 us -> 28.2 us  [the longest x1 11.1 us: per_device(): grad_up = summed(up_grad, both_acts).astype(jnp.bfloat16)[None]]
    reduce_scatter x1 -> x0, waiting for transfers between devices: 37.4 us -> none  [per_device(): lax.psum_scatter((jnp.dot(gate_grad, gate_local, preferred_element_type=j...]
    dot_general x4 -> x1, matrix products: 28.6 us -> 2.06 us  [contract_first(): lax.dot_general(left, right, (((0,), (0,)), ((), ())), preferred_element_...]
  transfers between devices with their start and end apart: 7 -> 2, of which waited for: 6 -> 0; matrix products, arithmetic and copies ran while one was open for 20% -> 17% of each run, Pallas kernels for 0% -> 0%
where the time goes in v2:
time: 170 us
  Pallas kernels  124 us (73%)
  matrix products  34.5 us (20%)
  starting transfers between devices  7.5 us (4%)
  other arithmetic  2.61 us (2%)
    pallas_call x1, Pallas kernels, exchange(): pl.pallas_call(functools.partial(exchange_kernel, n), out_shape=[both, bo...  124 us
    dot_general x1, matrix products, per_device(): grad_up = summed(up_grad, both_acts).astype(jnp.bfloat16)[None]  11.1 us
    dot_general x1, matrix products, per_device(): grad_gate = summed(gate_grad, both_acts).astype(jnp.bfloat16)[None]  8.61 us
    dot_general x1, matrix products, per_device(): grad_down = summed(hidden, both_grads).astype(jnp.bfloat16)[None]  8.53 us
    ppermute x2, starting transfers between devices, from_behind(): return lax.ppermute(block, axis, route)  7.5 us
  transfers between devices with their start and end apart: 2, of which 0 were waited for; matrix products, arithmetic and copies ran while one was open for 17% of the time, Pallas kernels for 0%

profile of v2, /device:TPU:17, one launch (start us, length us, event | category | flops | bytes accessed | tf_op | source)
XLA Modules:
  0.0 169.7 jit_solution(2002651463254593439)
XLA Ops:
  0.6 0.0 copy-start
  0.6 0.9 select_reduce_fusion
  1.5 0.3 reduce-window.9
  1.9 0.1 slice.7
  2.0 0.1 slice_reduce_fusion
  2.1 0.1 fusion.17
  2.2 0.1 copy-done
  2.3 1.3 convolution_convert_fusion.5.acts_in
  3.5 3.0 %convolution_convert_fusion.4.grads_in = bf16[64,4096]{1,0:T(8,128)(2,1)} fusion(bf16[1,1,256,4096]{3,2,1,0:T(8,128)(2,1)} %param.8, f32[256]{0:T(256)S(1)} %get-tuple-element.18, s32[256]{0:T(256)S(1)} %get-tuple-element.17, pred[256]{0:T(512)(128)(4,1)S(1)} %reduce_or.9), kind=kOutput, calls=%fused_computation.8 | convolution fusion | flops 137658368 | bytes 2623744 | tf_op jit(solution)/shard_map/dot_general | solution.py:350
  6.5 124.0 %shard_map.102 = (bf16[2,256,4096]{2,1,0:T(8,128)(2,1)}, bf16[2,256,4096]{2,1,0:T(8,128)(2,1)}, bf16[1344,512]{1,0:T(8,128)(2,1)}, bf16[1344,512]{1,0:T(8,128)(2...) custom-call(bf16[64,4096]{1,0:T(8,128)(2,1)} %convolution_convert_fusion.5.acts_in, ...), custom_call_target="tpu_custom_call" | custom-call | flops 22548578304 | bytes 44040192 | tf_op jit(solution)/shard_map/pallas_call | solution.py:305
  130.6 1.3 convert_element_type.58
  131.9 5.6 %collective-permute-start.1 = (bf16[64,4096]{1,0:T(8,128)(2,1)S(1)}, bf16[64,4096]{1,0:T(8,128)(2,1)S(1)}, u32[]{:S(2)}, u32[]{:S(2)}) collective-permute-start(bf16[64,4096]{1,0:T(8,128)(2,1)S(1)} %convert_element_type.58), channel_id=1, source_target_pairs={{4,0},{8,4},{12,8},{5,1},{9,5},{13,9},{6,2},{10,6},{14,10},{7,3},{... | collective-permute-start | bytes 1572872 | tf_op jit(solution)/shard_map/ppermute | solution.py:16
  137.4 1.9 %collective-permute-start = (bf16[256]{0:T(256)(128)(2,1)S(1)}, bf16[256]{0:T(256)(128)(2,1)S(1)}, u32[]{:S(2)}, u32[]{:S(2)}) collective-permute-start(bf16[256]{0:T(256)(128)(2,1)S(1)} %get-tuple-element.16), channel_id=1, source_target_pairs={{4,0},{8,4},{12,8},{5,1},{9,5},{13,9},{6,2},{10,6},{14,10},{7,3},{... | collective-permute-start | bytes 1544 | tf_op jit(solution)/shard_map/ppermute | solution.py:16
  139.4 0.0 copy-start.3
  139.4 0.0 copy-start.5
  139.4 11.1 %fusion.1 = bf16[1,1344,4096]{2,1,0:T(8,128)(2,1)} fusion(bf16[1344,512]{1,0:T(8,128)(2,1)} %get-tuple-element.12, bf16[512,4096]{1,0:T(8,128)(2,1)} %bitcast.38), kind=kOutput, calls=%fused_computation.4 | convolution fusion | flops 5642649600 | bytes 16580608 | tf_op jit(solution)/shard_map/dot_general | solution.py:386
  150.5 0.0 copy-done.3
  150.5 0.0 copy-done.5
  150.5 0.0 copy-start.2
  150.5 0.0 copy-start.4
  150.5 8.6 %fusion = bf16[1,1344,4096]{2,1,0:T(8,128)(2,1)} fusion(bf16[1344,512]{1,0:T(8,128)(2,1)S(1)} %copy-done.5, bf16[512,4096]{1,0:T(8,128)(2,1)S(1)} %bitcast.39), kind=kOutput, calls=%fused_computation.3 | convolution fusion | flops 5642649600 | bytes 16580608 | tf_op jit(solution)/shard_map/dot_general | solution.py:385
  159.1 0.0 copy-done.2
  159.1 0.0 copy-done.4
  159.1 0.0 copy-start.1
  159.1 8.5 %fusion.2 = bf16[1,1344,4096]{2,1,0:T(8,128)(2,1)} fusion(bf16[1344,512]{1,0:T(8,128)(2,1)S(1)} %copy-done.4, bf16[512,4096]{1,0:T(8,128)(2,1)S(1)} %bitcast.37), kind=kOutput, calls=%fused_computation.5 | convolution fusion | flops 5642649600 | bytes 16580608 | tf_op jit(solution)/shard_map/dot_general | solution.py:387
  167.6 0.0 collective-permute-done
  167.6 0.0 collective-permute-done.1
  167.6 2.1 %fusion.3 = bf16[1,1,256,4096]{3,2,1,0:T(8,128)(2,1)} fusion(bf16[64,4096]{1,0:T(8,128)(2,1)S(1)} %collective-permute-done.1, s32[256]{0:T(256)S(1)} %add_convert_fusion), kind=kOutput, calls=%fused_computation.7 | convolution fusion | flops 135282688 | bytes 2622464 | tf_op jit(solution)/shard_map/dot_general | solution.py:26
  169.7 0.0 copy-done.1
  (4 shorter events, 0.1 us)
Async XLA Ops:
  0.6 1.6 copy-start
  131.9 35.8 %collective-permute-start.1 = (bf16[64,4096]{1,0:T(8,128)(2,1)S(1)}, bf16[64,4096]{1,0:T(8,128)(2,1)S(1)}, u32[]{:S(2)}, u32[]{:S(2)}) collective-permute-start(bf16[64,4096]{1,0:T(8,128)(2,1)S(1)} %convert_element_type.58), channel_id=1, source_target_pairs={{4,0},{8,4},{12,8},{5,1},{9,5},{13,9},{6,2},{10,6},{14,10},{7,3},{... | collective-permute-start | bytes 1572872 | tf_op jit(solution)/shard_map/ppermute | solution.py:16
  137.4 30.2 %collective-permute-start = (bf16[256]{0:T(256)(128)(2,1)S(1)}, bf16[256]{0:T(256)(128)(2,1)S(1)}, u32[]{:S(2)}, u32[]{:S(2)}) collective-permute-start(bf16[256]{0:T(256)(128)(2,1)S(1)} %get-tuple-element.16), channel_id=1, source_target_pairs={{4,0},{8,4},{12,8},{5,1},{9,5},{13,9},{6,2},{10,6},{14,10},{7,3},{... | collective-permute-start | bytes 1544 | tf_op jit(solution)/shard_map/ppermute | solution.py:16
  139.4 11.1 %copy-start.3 = (bf16[2,256,4096]{2,1,0:T(8,128)(2,1)S(1)}, bf16[2,256,4096]{2,1,0:T(8,128)(2,1)}, u32[]{:S(2)}) copy-start(bf16[2,256,4096]{2,1,0:T(8,128)(2,1)} %get-tuple-element.11) | copy-start | bytes 12582916
  139.4 11.1 %copy-start.5 = (bf16[1344,512]{1,0:T(8,128)(2,1)S(1)}, bf16[1344,512]{1,0:T(8,128)(2,1)}, u32[]{:S(2)}) copy-start(bf16[1344,512]{1,0:T(8,128)(2,1)} %get-tuple-element.10) | copy-start | bytes 4128772
  150.5 8.6 %copy-start.2 = (bf16[2,256,4096]{2,1,0:T(8,128)(2,1)S(1)}, bf16[2,256,4096]{2,1,0:T(8,128)(2,1)}, u32[]{:S(2)}) copy-start(bf16[2,256,4096]{2,1,0:T(8,128)(2,1)} %get-tuple-element.14) | copy-start | bytes 12582916
  150.5 8.6 %copy-start.4 = (bf16[1344,512]{1,0:T(8,128)(2,1)S(1)}, bf16[1344,512]{1,0:T(8,128)(2,1)}, u32[]{:S(2)}) copy-start(bf16[1344,512]{1,0:T(8,128)(2,1)} %get-tuple-element.13) | copy-start | bytes 4128772
  159.1 10.6 %copy-start.1 = (bf16[1,1,256,4096]{3,2,1,0:T(8,128)(2,1)S(1)}, bf16[1,1,256,4096]{3,2,1,0:T(8,128)(2,1)}, u32[]{:S(2)}) copy-start(bf16[1,1,256,4096]{3,2,1,0:T(8,128)(2,1)} %param.7) | copy-start | bytes 6291460

commit v3 on v2

--- a/solution.py
+++ b/solution.py
@@ -48,10 +48,10 @@
 
 def exchange_kernel(
     n, acts_in, grads_in, gate_hbm, up_hbm, down_hbm,
-    acts_out, grads_out, hidden_o, gate_o, up_o, input_o,
-    acts_buf, grads_buf, gate_w, up_w, down_w, gate_t, up_t, part, from_low, from_high,
+    acts_out, grads_out, hidden_o, gate_o, up_o, part, next_up, next_down,
+    acts_buf, grads_buf, gate_w, up_w, down_w, gate_t, up_t, from_low, from_high,
     own_sem, weight_sem, out_sem, z_recv, up_send, down_send, x_recv, x_send,
-    low_recv, high_recv, sum_up_send, sum_down_send,
+    relay_send, low_recv, high_recv, sum_up_send, sum_down_send,
 ):
     i = lax.axis_index("dp")
     c = lax.axis_index("cuts")
@@ -62,6 +62,8 @@
     tile = hid // TILES
     bufs = (acts_buf, grads_buf)
     has_low, has_high = i > 0, i < n - 1
+    first, last = i == 0, i == n - 1
+    second, next_last = i == 1, i == n - 2
     low, high, across = {"dp": i - 1}, {"dp": i + 1}, {"cuts": other}
 
     weight_copies = [
@@ -124,6 +126,25 @@
             device_id_type=pl.DeviceIdType.MESH,
         )
 
+    def relay(kind, j, where):
+        return pltpu.make_async_remote_copy(
+            src_ref=slot(kind, other, j),
+            dst_ref=slot(kind, other, j),
+            send_sem=relay_send.at[kind],
+            recv_sem=x_recv.at[kind, j],
+            device_id=where,
+            device_id_type=pl.DeviceIdType.MESH,
+        )
+
+    def crosses(kind, d):
+        if d == 1:
+            relayed = jnp.logical_or(second, last) if kind else second
+            return jnp.logical_not(relayed)
+        if d == -1:
+            relayed = jnp.logical_or(next_last, first) if kind else next_last
+            return jnp.logical_not(relayed)
+        return i >= 0
+
     for kind in range(2):
         pl.when(has_high)(lambda kind=kind: to_high(kind, i).start())
         pl.when(has_low)(lambda kind=kind: to_low(kind, i).start())
@@ -137,13 +158,27 @@
             def _(kind=kind, d=d):
                 to_high(kind, i - d).wait_recv()
                 pl.when(has_high)(lambda: to_high(kind, i - d).start())
-                to_other(kind, i - d).start()
+                pl.when(crosses(kind, d))(lambda: to_other(kind, i - d).start())
 
             @pl.when(i + d < n)
             def _(kind=kind, d=d):
                 to_low(kind, i + d).wait_recv()
                 pl.when(has_low)(lambda: to_low(kind, i + d).start())
-                to_other(kind, i + d).start()
+                pl.when(crosses(kind, -d))(lambda: to_other(kind, i + d).start())
+
+        if d == 1:
+
+            @pl.when(first)
+            def _():
+                for kind in range(2):
+                    from_other(kind, 0).wait_recv()
+                    relay(kind, 0, high).start()
+
+            @pl.when(last)
+            def _():
+                for kind in range(2):
+                    from_other(kind, n - 1).wait_recv()
+                    relay(kind, n - 1, low).start()
 
     for copy in weight_copies:
         copy.wait()
@@ -183,103 +218,124 @@
     def share(j):
         return pl.ds(pl.multiple_of(j * cap, cap), cap)
 
-    def sum_high(j):
+    def sum_high():
         return pltpu.make_async_remote_copy(
-            src_ref=part.at[share(j), :],
-            dst_ref=from_low.at[j],
-            send_sem=sum_up_send.at[j],
-            recv_sem=low_recv.at[j],
+            src_ref=part.at[share(n - 1), :],
+            dst_ref=from_low,
+            send_sem=sum_up_send,
+            recv_sem=low_recv,
             device_id=high,
             device_id_type=pl.DeviceIdType.MESH,
         )
 
-    def sum_low(j):
+    def sum_low():
         return pltpu.make_async_remote_copy(
-            src_ref=part.at[share(j), :],
-            dst_ref=from_high.at[j],
-            send_sem=sum_down_send.at[j],
-            recv_sem=high_recv.at[j],
+            src_ref=part.at[share(0), :],
+            dst_ref=from_high,
+            send_sem=sum_down_send,
+            recv_sem=high_recv,
             device_id=low,
             device_id_type=pl.DeviceIdType.MESH,
         )
 
-    def add_to_part(arrived, j):
-        part[share(j), :] = (
-            part[share(j), :].astype(jnp.float32) + arrived[j].astype(jnp.float32)
+    pl.when(first)(lambda: sum_high().start())
+    pl.when(last)(lambda: sum_low().start())
+
+    @pl.when(second)
+    def _():
+        to_low(1, n - 1).wait_send()
+        from_other(1, 1).wait_recv()
+        relay(1, 1, low).start()
+
+    @pl.when(next_last)
+    def _():
+        to_high(1, 0).wait_send()
+        from_other(1, n - 2).wait_recv()
+        relay(1, n - 2, high).start()
+
+    for j in range(n):
+        for kind in range(2):
+            seen = []
+            if j == 0:
+                seen.append(first)
+            if j == n - 1:
+                seen.append(last)
+            if kind == 1 and j == 1:
+                seen.append(second)
+            if kind == 1 and j == n - 2:
+                seen.append(next_last)
+            if seen:
+                pl.when(jnp.logical_not(functools.reduce(jnp.logical_or, seen)))(
+                    lambda kind=kind, j=j: from_other(kind, j).wait_recv()
+                )
+            else:
+                from_other(kind, j).wait_recv()
+    out_copies = [
+        pltpu.make_async_copy(acts_buf, acts_out, out_sem.at[0]),
+        pltpu.make_async_copy(grads_buf, grads_out, out_sem.at[1]),
+    ]
+    for copy in out_copies:
+        copy.start()
+
+    @pl.loop(0, TILES)
+    def _(t):
+        forward(other, t)
+
+    next_up[...] = part[share(lax.rem(i + n - 2, n)), :]
+    next_down[...] = part[share(lax.rem(i + 2, n)), :]
+
+    @pl.when(second)
+    def _():
+        sum_high().wait_recv()
+        next_up[...] = (
+            next_up[...].astype(jnp.float32) + from_low[...].astype(jnp.float32)
         ).astype(jnp.bfloat16)
 
-    def pass_up(j):
-        @pl.when(i < j)
-        def _():
-            @pl.when(has_low)
-            def _():
-                sum_high(j).wait_recv()
-                add_to_part(from_low, j)
-
-            sum_high(j).start()
-
-    def pass_down(j):
-        @pl.when(i > j)
-        def _():
-            @pl.when(has_high)
-            def _():
-                sum_low(j).wait_recv()
-                add_to_part(from_high, j)
-
-            sum_low(j).start()
-
-    lower_half = 2 * i < n
-    for k in range(n - 1):
-
-        @pl.when(lower_half)
-        def _(k=k):
-            pass_up(n - 1 - k)
-            pass_down(k)
-
-        @pl.when(jnp.logical_not(lower_half))
-        def _(k=k):
-            pass_down(k)
-            pass_up(n - 1 - k)
-
-        if k == 0:
-            for j in range(n):
-                for kind in range(2):
-                    from_other(kind, j).wait_recv()
-            out_copies = [
-                pltpu.make_async_copy(acts_buf, acts_out, out_sem.at[0]),
-                pltpu.make_async_copy(grads_buf, grads_out, out_sem.at[1]),
-            ]
-            for copy in out_copies:
-                copy.start()
-        if k < TILES:
-            forward(other, k)
-    for k in range(n - 1, TILES):
-        forward(other, k)
-
-    total = part[share(i), :].astype(jnp.float32)
-    input_o[...] = total
-
-    @pl.when(has_low)
+    @pl.when(next_last)
     def _():
-        sum_high(i).wait_recv()
-        input_o[...] += from_low[i].astype(jnp.float32)
-
-    @pl.when(has_high)
+        sum_low().wait_recv()
+        next_down[...] = (
+            next_down[...].astype(jnp.float32) + from_high[...].astype(jnp.float32)
+        ).astype(jnp.bfloat16)
+
+    pl.when(first)(lambda: sum_high().wait_send())
+    pl.when(last)(lambda: sum_low().wait_send())
+
+    @pl.when(first)
     def _():
-        sum_low(i).wait_recv()
-        input_o[...] += from_high[i].astype(jnp.float32)
-
-    for j in range(n):
-        pl.when(i < j)(lambda j=j: sum_high(j).wait_send())
-        pl.when(i > j)(lambda j=j: sum_low(j).wait_send())
         for kind in range(2):
-            to_other(kind, j).wait_send()
-            pl.when(jnp.logical_and(has_high, i >= j))(
-                lambda kind=kind, j=j: to_high(kind, j).wait_send()
-            )
-            pl.when(jnp.logical_and(has_low, i <= j))(
-                lambda kind=kind, j=j: to_low(kind, j).wait_send()
-            )
+            relay(kind, 0, high).wait_send()
+
+    @pl.when(last)
+    def _():
+        for kind in range(2):
+            relay(kind, n - 1, low).wait_send()
+
+    pl.when(second)(lambda: relay(1, 1, low).wait_send())
+    pl.when(next_last)(lambda: relay(1, n - 2, high).wait_send())
+    for kind in range(2):
+        to_other(kind, i).wait_send()
+        pl.when(has_high)(lambda kind=kind: to_high(kind, i).wait_send())
+        pl.when(has_low)(lambda kind=kind: to_low(kind, i).wait_send())
+    for d in range(1, n):
+        for kind in range(2):
+
+            @pl.when(i - d >= 0)
+            def _(kind=kind, d=d):
+                early = jnp.logical_and(next_last, jnp.bool_(kind == 1 and d == n - 2))
+                pl.when(jnp.logical_and(has_high, jnp.logical_not(early)))(
+                    lambda: to_high(kind, i - d).wait_send()
+                )
+                pl.when(crosses(kind, d))(lambda: to_other(kind, i - d).wait_send())
+
+            @pl.when(i + d < n)
+            def _(kind=kind, d=d):
+                early = jnp.logical_and(second, jnp.bool_(kind == 1 and d == n - 2))
+                pl.when(jnp.logical_and(has_low, jnp.logical_not(early)))(
+                    lambda: to_low(kind, i + d).wait_send()
+                )
+                pl.when(crosses(kind, -d))(lambda: to_other(kind, i + d).wait_send())
+
     for copy in out_copies:
         copy.wait()
 
@@ -305,9 +361,11 @@
     return pl.pallas_call(
         functools.partial(exchange_kernel, n),
         out_shape=[both, both, units, units, units,
-                   jax.ShapeDtypeStruct((cap, width), jnp.float32)],
+                   jax.ShapeDtypeStruct((rows, width), bf16),
+                   jax.ShapeDtypeStruct((cap, width), bf16),
+                   jax.ShapeDtypeStruct((cap, width), bf16)],
         in_specs=[anywhere] * 5,
-        out_specs=[anywhere, anywhere, vmem, vmem, vmem, vmem],
+        out_specs=[anywhere, anywhere] + [vmem] * 6,
         scratch_shapes=[
             pltpu.VMEM((2, rows, width), bf16),
             pltpu.VMEM((2, rows, width), bf16),
@@ -316,12 +374,11 @@
             pltpu.VMEM((hid, width), bf16),
             pltpu.VMEM((rows, hid), bf16),
             pltpu.VMEM((rows, hid), bf16),
-            pltpu.VMEM((rows, width), bf16),
-            pltpu.VMEM((n, cap, width), bf16),
-            pltpu.VMEM((n, cap, width), bf16),
+            pltpu.VMEM((cap, width), bf16),
+            pltpu.VMEM((cap, width), bf16),
             dma((2,)), dma((3,)), dma((2,)),
             dma((2, n)), dma((2, n)), dma((2, n)), dma((2, n)), dma((2, n)),
-            dma((n,)), dma((n,)), dma((n,)), dma((n,)),
+            dma((2,)), dma, dma, dma, dma,
         ],
         compiler_params=pltpu.CompilerParams(
             collective_id=0, has_side_effects=True, vmem_limit_bytes=VMEM_BUDGET
@@ -330,6 +387,38 @@
             flops=16 * rows * hid * width, bytes_accessed=8 * hid * width, transcendentals=0
         ),
     )(acts, grads, gate_local, up_local, down_local)
+
+
+def chained_sum(n, part, up, down):
+    i = lax.axis_index("dp")
+    sections = range(lax.axis_size("section"))
+    shares = part.reshape(n, CAP, part.shape[1])
+
+    def mine(j):
+        return lax.dynamic_index_in_dim(shares, jnp.clip(j, 0, n - 1), keepdims=False)
+
+    def hop(block, senders, step, back):
+        pairs = [
+            (s * n + k, (s - back) * n + k + step)
+            for s in sections
+            for k in senders
+            if s >= back
+        ]
+        return lax.ppermute(block, ("section", "dp"), pairs)
+
+    def joined(left, right):
+        return (left.astype(jnp.float32) + right.astype(jnp.float32)).astype(jnp.bfloat16)
+
+    for t in range(2, n):
+        if t > 2:
+            up = joined(up, mine(i + n - t))
+            down = joined(down, mine(i - n + t))
+        back = int(t == n - 1)
+        up = hop(up, range(t), 1, back)
+        down = hop(down, range(n - t, n), -1, back)
+    own = hop(mine(i), range(n), 0, 1)
+    total = own.astype(jnp.float32) + up.astype(jnp.float32) + down.astype(jnp.float32)
+    return total.astype(jnp.bfloat16)
 
 
 def per_device(
@@ -353,11 +442,11 @@
     down_local = down_weight[0]
     n = lax.axis_size("dp")
     hid, width = gate_local.shape
-    if kernel_bytes(n, CAP, hid, width) <= VMEM_BUDGET and hid % (16 * TILES) == 0:
-        acts, grads, hidden, gate_grad, up_grad, input_rows = exchange(
+    if kernel_bytes(n, CAP, hid, width) <= VMEM_BUDGET and hid % (16 * TILES) == 0 and n >= 4:
+        acts, grads, hidden, gate_grad, up_grad, part, next_up, next_down = exchange(
             n, packed_acts, packed_grads, gate_local, up_local, down_local
         )
-        input_rows = input_rows.astype(jnp.bfloat16)
+        behind_rows = chained_sum(n, part, next_up, next_down)
         both_acts = acts.reshape(2 * n * CAP, width)
         both_grads = grads.reshape(2 * n * CAP, width)
         summed = functools.partial(jnp.dot, preferred_element_type=jnp.float32)
@@ -381,12 +470,12 @@
         hidden, gate_grad, up_grad = hidden_backward(
             both_acts, both_grads, gate_local, up_local, down_local
         )
+        behind_rows = from_behind(input_rows, "section", -1)
         summed = contract_first
     grad_gate = summed(gate_grad, both_acts).astype(jnp.bfloat16)[None]
     grad_up = summed(up_grad, both_acts).astype(jnp.bfloat16)[None]
     grad_down = summed(hidden, both_grads).astype(jnp.bfloat16)[None]
     slot = jnp.where(is_routed, row_index, -1).astype(jnp.bfloat16)
-    behind_rows = from_behind(input_rows, "section", -1)
     behind_slot = from_behind(slot + 1.0, "section", -1) - 1.0
     behind_picker = (
         behind_slot[None, :].astype(jnp.int32) == wanted[:, None]

time: 170 us -> 166 us (0.976)
  Pallas kernels: 124 us -> 105 us
  starting transfers between devices: 7.5 us -> 14.5 us
  waiting for transfers between devices: 0.01 us -> 3.86 us
  matrix products: 34.5 us -> 37 us
    pallas_call x1, Pallas kernels: 124 us -> 105 us  [exchange(): pl.pallas_call(functools.partial(exchange_kernel, n), out_shape=[both, bo...]
    ppermute x0 -> x5, starting transfers between devices: none -> 11.9 us  [hop(): return lax.ppermute(block, ('section', 'dp'), pairs)]
    ppermute x2 -> x1, starting transfers between devices: 7.5 us -> 2.57 us  [from_behind(): return lax.ppermute(block, axis, route)]
    ppermute x0 -> x5, waiting for transfers between devices: none -> 3.86 us  [hop(): return lax.ppermute(block, ('section', 'dp'), pairs)]
    dot_general x1, matrix products: 8.53 us -> 11.1 us  [per_device(): grad_down = summed(hidden, both_grads).astype(jnp.bfloat16)[None]]
  transfers between devices with their start and end apart: 2 -> 6, of which waited for: 0 -> 2; matrix products, arithmetic and copies ran while one was open for 17% -> 23% of each run, Pallas kernels for 0% -> 63%
where the time goes in v3:
time: 166 us; the launch traced here: 165 us
  Pallas kernels  105 us (63%)
  matrix products  37 us (22%)
  starting transfers between devices  14.5 us (9%)
  waiting for transfers between devices  3.86 us (2%)
  other arithmetic  2.78 us (2%)
    pallas_call x1, Pallas kernels, exchange(): pl.pallas_call(functools.partial(exchange_kernel, n), out_shape=[both, bo...  105 us
    ppermute x5, starting transfers between devices, hop(): return lax.ppermute(block, ('section', 'dp'), pairs)  11.9 us
    dot_general x1, matrix products, per_device(): grad_up = summed(up_grad, both_acts).astype(jnp.bfloat16)[None]  11.1 us
    dot_general x1, matrix products, per_device(): grad_down = summed(hidden, both_grads).astype(jnp.bfloat16)[None]  11.1 us
    dot_general x1, matrix products, per_device(): grad_gate = summed(gate_grad, both_acts).astype(jnp.bfloat16)[None]  8.53 us
    ppermute x5, waiting for transfers between devices, hop(): return lax.ppermute(block, ('section', 'dp'), pairs)  3.86 us
  transfers between devices with their start and end apart: 6, of which 2 were waited for; matrix products, arithmetic and copies ran while one was open for 23% of the time, Pallas kernels for 63%

profile of v3, /device:TPU:17, one launch (start us, length us, event | category | flops | bytes accessed | tf_op | source)
XLA Modules:
  0.0 164.8 jit_solution(8838186098545079184)
XLA Ops:
  0.6 0.0 copy-start
  0.6 0.9 select_reduce_fusion
  1.5 0.3 reduce-window.9
  1.9 0.1 slice.7
  2.0 0.1 slice_reduce_fusion
  2.1 0.1 fusion.19
  2.2 2.6 %collective-permute-start = (bf16[256]{0:T(256)(128)(2,1)S(1)}, bf16[256]{0:T(256)(128)(2,1)S(1)}, u32[]{:S(2)}, u32[]{:S(2)}) collective-permute-start(bf16[256]{0:T(256)(128)(2,1)S(1)} %get-tuple-element.20), channel_id=1, source_target_pairs={{4,0},{8,4},{12,8},{5,1},{9,5},{13,9},{6,2},{10,6},{14,10},{7,3},{... | collective-permute-start | bytes 1544 | tf_op jit(solution)/shard_map/ppermute | solution.py:16
  4.8 0.0 copy-done
  4.8 1.3 convolution_convert_fusion.5.acts_in
  6.0 3.0 %convolution_convert_fusion.4.grads_in = bf16[64,4096]{1,0:T(8,128)(2,1)} fusion(bf16[1,1,256,4096]{3,2,1,0:T(8,128)(2,1)} %param.8, f32[256]{0:T(256)S(1)} %get-tuple-element.22, s32[256]{0:T(256)S(1)} %get-tuple-element.21, pred[256]{0:T(512)(128)(4,1)S(1)} %reduce_or.9), kind=kOutput, calls=%fused_computation.8 | convolution fusion | flops 137658368 | bytes 2623744 | tf_op jit(solution)/shard_map/dot_general | solution.py:439
  9.0 104.6 %shard_map.102 = (bf16[2,256,4096]{2,1,0:T(8,128)(2,1)}, bf16[2,256,4096]{2,1,0:T(8,128)(2,1)}, bf16[1344,512]{1,0:T(8,128)(2,1)}, bf16[1344,512]{1,0:T(8,128)(2...) custom-call(bf16[64,4096]{1,0:T(8,128)(2,1)} %convolution_convert_fu, ...), custom_call_target="tpu_custom_call" | custom-call | flops 22548578304 | bytes 44040192 | tf_op jit(solution)/shard_map/pallas_call | solution.py:361
  113.6 1.1 dynamic-slice_bitcast_fusion
  114.7 2.6 %collective-permute-start.1 = (bf16[64,4096]{1,0:T(8,128)(2,1)S(1)}, bf16[64,4096]{1,0:T(8,128)(2,1)S(1)}, u32[]{:S(2)}, u32[]{:S(2)}) collective-permute-start(bf16[64,4096]{1,0:T(8,128)(2,1)S(1)} %dynamic-slice_bitcast_fusion), channel_id=1, source_target_pairs={{4,0},{5,1},{6,2},{7,3},{8,4},{9,5},{10,6},{11,7},{12,8},{13,9},{1... | collective-permute-start | bytes 1572872 | tf_op jit(solution)/shard_map/ppermute | solution.py:407
  117.3 1.3 collective-permute-start.2
  118.6 4.2 %collective-permute-start.4 = (bf16[64,4096]{1,0:T(8,128)(2,1)}, bf16[64,4096]{1,0:T(8,128)(2,1)}, u32[]{:S(2)}, u32[]{:S(2)}) collective-permute-start(bf16[64,4096]{1,0:T(8,128)(2,1)} %get-tuple-element.19), channel_id=1, source_target_pairs={{2,1},{3,2},{6,5},{7,6},{10,9},{11,10},{14,13},{15,14},{18,17},{19... | collective-permute-start | bytes 1572872 | tf_op jit(solution)/shard_map/ppermute | solution.py:407
  122.8 0.0 copy-start.3
  122.8 11.1 %fusion.1 = bf16[1,1344,4096]{2,1,0:T(8,128)(2,1)} fusion(bf16[1344,512]{1,0:T(8,128)(2,1)} %get-tuple-element.14, bf16[512,4096]{1,0:T(8,128)(2,1)} %bitcast.48), kind=kOutput, calls=%fused_computation.4 | convolution fusion | flops 5642649600 | bytes 16580608 | tf_op jit(solution)/shard_map/dot_general | solution.py:476
  133.9 8.5 %fusion = bf16[1,1344,4096]{2,1,0:T(8,128)(2,1)} fusion(bf16[1344,512]{1,0:T(8,128)(2,1)S(1)} %copy-done.4, bf16[512,4096]{1,0:T(8,128)(2,1)S(1)} %bitcast.49), kind=kOutput, calls=%fused_computation.3 | convolution fusion | flops 5642649600 | bytes 16580608 | tf_op jit(solution)/shard_map/dot_general | solution.py:475
  142.4 0.0 collective-permute-done.2
  142.4 0.0 collective-permute-done.4
  142.4 0.0 copy-done.2
  142.4 1.4 fusion.10
  143.9 1.9 %collective-permute-start.3 = (bf16[64,4096]{1,0:T(8,128)(2,1)S(1)}, bf16[64,4096]{1,0:T(8,128)(2,1)S(1)}, u32[]{:S(2)}, u32[]{:S(2)}) collective-permute-start(bf16[64,4096]{1,0:T(8,128)(2,1)S(1)} %get-tuple-element.24), channel_id=1, source_target_pairs={{4,1},{5,2},{6,3},{8,5},{9,6},{10,7},{12,9},{13,10},{14,11},{20,17... | collective-permute-start | bytes 1572872 | tf_op jit(solution)/shard_map/ppermute | solution.py:407
  145.8 1.9 %collective-permute-start.5 = (bf16[64,4096]{1,0:T(8,128)(2,1)S(1)}, bf16[64,4096]{1,0:T(8,128)(2,1)S(1)}, u32[]{:S(2)}, u32[]{:S(2)}) collective-permute-start(bf16[64,4096]{1,0:T(8,128)(2,1)S(1)} %get-tuple-element.25), channel_id=1, source_target_pairs={{5,0},{6,1},{7,2},{9,4},{10,5},{11,6},{13,8},{14,9},{15,10},{21,16... | collective-permute-start | bytes 1572872 | tf_op jit(solution)/shard_map/ppermute | solution.py:407
  147.8 0.0 copy-start.1
  147.8 11.1 %fusion.2 = bf16[1,1344,4096]{2,1,0:T(8,128)(2,1)} fusion(bf16[1344,512]{1,0:T(8,128)(2,1)} %get-tuple-element.15, bf16[512,4096]{1,0:T(8,128)(2,1)} %bitcast.47), kind=kOutput, calls=%fused_computation.5 | convolution fusion | flops 5642649600 | bytes 16580608 | tf_op jit(solution)/shard_map/dot_general | solution.py:477
  158.8 0.0 collective-permute-done
  158.8 0.0 collective-permute-done.1
  158.9 2.0 %collective-permute-done.3 = bf16[64,4096]{1,0:T(8,128)(2,1)S(1)} collective-permute-done((bf16[64,4096]{1,0:T(8,128)(2,1)S(1)}, bf16[64,4096]{1,0:T(8,128)(2,1)S(1)}, u32[]{:S(2)}, u32[]{:S(2)}) %collective-permute-start.3) | collective-permute-done | bytes 524320 | tf_op jit(solution)/shard_map/ppermute | solution.py:407
  160.8 1.9 %collective-permute-done.5 = bf16[64,4096]{1,0:T(8,128)(2,1)S(1)} collective-permute-done((bf16[64,4096]{1,0:T(8,128)(2,1)S(1)}, bf16[64,4096]{1,0:T(8,128)(2,1)S(1)}, u32[]{:S(2)}, u32[]{:S(2)}) %collective-permute-start.5) | collective-permute-done | bytes 524320 | tf_op jit(solution)/shard_map/ppermute | solution.py:407
  162.7 2.1 %fusion.3 = bf16[1,1,256,4096]{3,2,1,0:T(8,128)(2,1)} fusion(bf16[64,4096]{1,0:T(8,128)(2,1)S(1)} %collective-permute-done.5, bf16[64,4096]{1,0:T(8,128)(2,1)S(1)} %collective-permute-done.3, bf16[64,4096]{1,0:T(8,128)(2,1)S(1)} %collective-permute-done.1, s32[256]{0:T(256)S(1)} %add_convert_fusion.2), kind=kOutput, calls=%fused_computation.7 | convolution fusion | flops 136855552 | bytes 3671040 | tf_op jit(solution)/shard_map/dot_general | solution.py:26
  164.8 0.0 copy-done.1
  (8 shorter events, 0.1 us)
Async XLA Ops:
  0.6 4.1 %copy-start = (bf16[1,1,256,4096]{3,2,1,0:T(8,128)(2,1)S(1)}, bf16[1,1,256,4096]{3,2,1,0:T(8,128)(2,1)}, u32[]{:S(2)}) copy-start(bf16[1,1,256,4096]{3,2,1,0:T(8,128)(2,1)} %param.7) | copy-start | bytes 6291460
  2.2 156.7 %collective-permute-start = (bf16[256]{0:T(256)(128)(2,1)S(1)}, bf16[256]{0:T(256)(128)(2,1)S(1)}, u32[]{:S(2)}, u32[]{:S(2)}) collective-permute-start(bf16[256]{0:T(256)(128)(2,1)S(1)} %get-tuple-element.20), channel_id=1, source_target_pairs={{4,0},{8,4},{12,8},{5,1},{9,5},{13,9},{6,2},{10,6},{14,10},{7,3},{... | collective-permute-start | bytes 1544 | tf_op jit(solution)/shard_map/ppermute | solution.py:16
  114.7 44.2 %collective-permute-start.1 = (bf16[64,4096]{1,0:T(8,128)(2,1)S(1)}, bf16[64,4096]{1,0:T(8,128)(2,1)S(1)}, u32[]{:S(2)}, u32[]{:S(2)}) collective-permute-start(bf16[64,4096]{1,0:T(8,128)(2,1)S(1)} %dynamic-slice_bitcast_fusion), channel_id=1, source_target_pairs={{4,0},{5,1},{6,2},{7,3},{8,4},{9,5},{10,6},{11,7},{12,8},{13,9},{1... | collective-permute-start | bytes 1572872 | tf_op jit(solution)/shard_map/ppermute | solution.py:407
  117.3 25.1 %collective-permute-start.2 = (bf16[64,4096]{1,0:T(8,128)(2,1)}, bf16[64,4096]{1,0:T(8,128)(2,1)}, u32[]{:S(2)}, u32[]{:S(2)}) collective-permute-start(bf16[64,4096]{1,0:T(8,128)(2,1)} %get-tuple-element.18), channel_id=1, source_target_pairs={{0,1},{1,2},{4,5},{5,6},{8,9},{9,10},{12,13},{13,14},{16,17},{17,1... | collective-permute-start | bytes 1572872 | tf_op jit(solution)/shard_map/ppermute | solution.py:407
  118.6 23.8 %collective-permute-start.4 = (bf16[64,4096]{1,0:T(8,128)(2,1)}, bf16[64,4096]{1,0:T(8,128)(2,1)}, u32[]{:S(2)}, u32[]{:S(2)}) collective-permute-start(bf16[64,4096]{1,0:T(8,128)(2,1)} %get-tuple-element.19), channel_id=1, source_target_pairs={{2,1},{3,2},{6,5},{7,6},{10,9},{11,10},{14,13},{15,14},{18,17},{19... | collective-permute-start | bytes 1572872 | tf_op jit(solution)/shard_map/ppermute | solution.py:407
  122.8 11.1 %copy-start.3 = (bf16[2,256,4096]{2,1,0:T(8,128)(2,1)S(1)}, bf16[2,256,4096]{2,1,0:T(8,128)(2,1)}, u32[]{:S(2)}) copy-start(bf16[2,256,4096]{2,1,0:T(8,128)(2,1)} %get-tuple-element.13) | copy-start | bytes 12582916
  122.8 11.1 %copy-start.4 = (bf16[1344,512]{1,0:T(8,128)(2,1)S(1)}, bf16[1344,512]{1,0:T(8,128)(2,1)}, u32[]{:S(2)}) copy-start(bf16[1344,512]{1,0:T(8,128)(2,1)} %get-tuple-element.12) | copy-start | bytes 4128772
  133.9 8.5 %copy-start.2 = (bf16[256,4096]{1,0:T(8,128)(2,1)S(1)}, bf16[256,4096]{1,0:T(8,128)(2,1)}, u32[]{:S(2)}) copy-start(bf16[256,4096]{1,0:T(8,128)(2,1)} %get-tuple-element.17) | copy-start | bytes 6291460
  143.9 16.9 %collective-permute-start.3 = (bf16[64,4096]{1,0:T(8,128)(2,1)S(1)}, bf16[64,4096]{1,0:T(8,128)(2,1)S(1)}, u32[]{:S(2)}, u32[]{:S(2)}) collective-permute-start(bf16[64,4096]{1,0:T(8,128)(2,1)S(1)} %get-tuple-element.24), channel_id=1, source_target_pairs={{4,1},{5,2},{6,3},{8,5},{9,6},{10,7},{12,9},{13,10},{14,11},{20,17... | collective-permute-start | bytes 1572872 | tf_op jit(solution)/shard_map/ppermute | solution.py:407
  145.8 16.9 %collective-permute-start.5 = (bf16[64,4096]{1,0:T(8,128)(2,1)S(1)}, bf16[64,4096]{1,0:T(8,128)(2,1)S(1)}, u32[]{:S(2)}, u32[]{:S(2)}) collective-permute-start(bf16[64,4096]{1,0:T(8,128)(2,1)S(1)} %get-tuple-element.25), channel_id=1, source_target_pairs={{5,0},{6,1},{7,2},{9,4},{10,5},{11,6},{13,8},{14,9},{15,10},{21,16... | collective-permute-start | bytes 1572872 | tf_op jit(solution)/shard_map/ppermute | solution.py:407
  147.8 17.0 %copy-start.1 = (bf16[1,1,256,4096]{3,2,1,0:T(8,128)(2,1)S(1)}, bf16[1,1,256,4096]{3,2,1,0:T(8,128)(2,1)}, u32[]{:S(2)}) copy-start(bf16[1,1,256,4096]{3,2,1,0:T(8,128)(2,1)} %param.7) | copy-start | bytes 6291460

commit v4 on v3

--- a/solution.py
+++ b/solution.py
@@ -49,8 +49,8 @@
 def exchange_kernel(
     n, acts_in, grads_in, gate_hbm, up_hbm, down_hbm,
     acts_out, grads_out, hidden_o, gate_o, up_o, part, next_up, next_down,
-    acts_buf, grads_buf, gate_w, up_w, down_w, gate_t, up_t, from_low, from_high,
-    own_sem, weight_sem, out_sem, z_recv, up_send, down_send, x_recv, x_send,
+    acts_buf, grads_buf, gate_w, up_w, down_w, gate_t, up_t, gate_pre, up_pre,
+    from_low, from_high, own_sem, weight_sem, out_sem, z_recv, up_send, down_send, x_recv, x_send,
     relay_send, low_recv, high_recv, sum_up_send, sum_down_send,
 ):
     i = lax.axis_index("dp")
@@ -145,62 +145,100 @@
             return jnp.logical_not(relayed)
         return i >= 0
 
-    for kind in range(2):
-        pl.when(has_high)(lambda kind=kind: to_high(kind, i).start())
-        pl.when(has_low)(lambda kind=kind: to_low(kind, i).start())
-        to_other(kind, i).start()
+    def prepare(replica, t):
+        some = pl.ds(pl.multiple_of(t * tile, tile), tile)
+        cols = pl.ds(pl.multiple_of(replica * rows, rows), rows)
+        gate_pre[some, cols] = contract_last(gate_w[some, :], acts_buf[replica])
+        up_pre[some, cols] = contract_last(up_w[some, :], acts_buf[replica])
+
+    def finish(replica, t):
+        some = pl.ds(pl.multiple_of(t * tile, tile), tile)
+        cols = pl.ds(pl.multiple_of(replica * rows, rows), rows)
+        hidden_grad = contract_last(down_w[some, :], grads_buf[replica])
+        gate, up = gate_pre[some, cols], up_pre[some, cols]
+        sig = jax.nn.sigmoid(gate)
+        silu = gate * sig
+        hidden_o[some, cols] = (silu * up).astype(jnp.bfloat16)
+        gate_o[some, cols] = (
+            hidden_grad * up * sig * (1.0 + gate * (1.0 - sig))
+        ).astype(jnp.bfloat16)
+        up_o[some, cols] = (hidden_grad * silu).astype(jnp.bfloat16)
+
+    def receive(kind, d):
+        @pl.when(i - d >= 0)
+        def _():
+            to_high(kind, i - d).wait_recv()
+            pl.when(has_high)(lambda: to_high(kind, i - d).start())
+            pl.when(crosses(kind, d))(lambda: to_other(kind, i - d).start())
+
+        @pl.when(i + d < n)
+        def _():
+            to_low(kind, i + d).wait_recv()
+            pl.when(has_low)(lambda: to_low(kind, i + d).start())
+            pl.when(crosses(kind, -d))(lambda: to_other(kind, i + d).start())
+
+    def relay_ends(kind):
+        @pl.when(first)
+        def _():
+            from_other(kind, 0).wait_recv()
+            relay(kind, 0, high).start()
+
+        @pl.when(last)
+        def _():
+            from_other(kind, n - 1).wait_recv()
+            relay(kind, n - 1, low).start()
+
+    def await_other(kind, j):
+        seen = []
+        if j == 0:
+            seen.append(first)
+        if j == n - 1:
+            seen.append(last)
+        if kind == 1 and j == 1:
+            seen.append(second)
+        if kind == 1 and j == n - 2:
+            seen.append(next_last)
+        if seen:
+            pl.when(jnp.logical_not(functools.reduce(jnp.logical_or, seen)))(
+                lambda: from_other(kind, j).wait_recv()
+            )
+        else:
+            from_other(kind, j).wait_recv()
+
+    pl.when(has_high)(lambda: to_high(0, i).start())
+    pl.when(has_low)(lambda: to_low(0, i).start())
+    to_other(0, i).start()
     for copy in weight_copies:
         copy.start()
-    for d in range(1, n):
-        for kind in range(2):
-
-            @pl.when(i - d >= 0)
-            def _(kind=kind, d=d):
-                to_high(kind, i - d).wait_recv()
-                pl.when(has_high)(lambda: to_high(kind, i - d).start())
-                pl.when(crosses(kind, d))(lambda: to_other(kind, i - d).start())
-
-            @pl.when(i + d < n)
-            def _(kind=kind, d=d):
-                to_low(kind, i + d).wait_recv()
-                pl.when(has_low)(lambda: to_low(kind, i + d).start())
-                pl.when(crosses(kind, -d))(lambda: to_other(kind, i + d).start())
-
+    for d in range(n):
+        if d > 0:
+            receive(0, d)
         if d == 1:
-
-            @pl.when(first)
-            def _():
-                for kind in range(2):
-                    from_other(kind, 0).wait_recv()
-                    relay(kind, 0, high).start()
-
-            @pl.when(last)
-            def _():
-                for kind in range(2):
-                    from_other(kind, n - 1).wait_recv()
-                    relay(kind, n - 1, low).start()
-
+            relay_ends(0)
+        pl.when(jnp.logical_and(has_high, i == d))(lambda: to_high(1, i).start())
+        pl.when(jnp.logical_and(has_low, i == n - 1 - d))(lambda: to_low(1, i).start())
+    to_other(1, i).start()
     for copy in weight_copies:
         copy.wait()
 
-    def forward(replica, t):
-        some = pl.ds(pl.multiple_of(t * tile, tile), tile)
-        cols = pl.ds(pl.multiple_of(replica * rows, rows), rows)
-        acts = acts_buf[replica]
-        gate_pre = contract_last(gate_w[some, :], acts)
-        up_pre = contract_last(up_w[some, :], acts)
-        hidden_grad = contract_last(down_w[some, :], grads_buf[replica])
-        sig = jax.nn.sigmoid(gate_pre)
-        silu = gate_pre * sig
-        hidden_o[some, cols] = (silu * up_pre).astype(jnp.bfloat16)
-        gate_o[some, cols] = (
-            hidden_grad * up_pre * sig * (1.0 + gate_pre * (1.0 - sig))
-        ).astype(jnp.bfloat16)
-        up_o[some, cols] = (hidden_grad * silu).astype(jnp.bfloat16)
+    todo = [(c, t) for t in range(TILES)] + [(other, t) for t in range(TILES)]
+    for d in range(1, n):
+        for _ in range(2):
+            if todo:
+                replica, t = todo.pop(0)
+                if replica is other and t == 0:
+                    for j in range(n):
+                        await_other(0, j)
+                prepare(replica, t)
+        receive(1, d)
+        if d == 2:
+            relay_ends(1)
+    for replica, t in todo:
+        prepare(replica, t)
 
     @pl.loop(0, TILES)
     def _(t):
-        forward(c, t)
+        finish(c, t)
 
     own_cols = pl.ds(pl.multiple_of(c * rows, rows), rows)
     gate_t[...] = jnp.transpose(gate_o[:, own_cols])
@@ -254,22 +292,7 @@
         relay(1, n - 2, high).start()
 
     for j in range(n):
-        for kind in range(2):
-            seen = []
-            if j == 0:
-                seen.append(first)
-            if j == n - 1:
-                seen.append(last)
-            if kind == 1 and j == 1:
-                seen.append(second)
-            if kind == 1 and j == n - 2:
-                seen.append(next_last)
-            if seen:
-                pl.when(jnp.logical_not(functools.reduce(jnp.logical_or, seen)))(
-                    lambda kind=kind, j=j: from_other(kind, j).wait_recv()
-                )
-            else:
-                from_other(kind, j).wait_recv()
+        await_other(1, j)
     out_copies = [
         pltpu.make_async_copy(acts_buf, acts_out, out_sem.at[0]),
         pltpu.make_async_copy(grads_buf, grads_out, out_sem.at[1]),
@@ -279,7 +302,7 @@
 
     @pl.loop(0, TILES)
     def _(t):
-        forward(other, t)
+        finish(other, t)
 
     next_up[...] = part[share(lax.rem(i + n - 2, n)), :]
     next_down[...] = part[share(lax.rem(i + 2, n)), :]
@@ -343,7 +366,7 @@
 def kernel_bytes(n, cap, hid, width):
     weights = 3 * hid * width * 2
     rows = 4 * n * cap * width * 2
-    hidden = (6 + 2) * hid * n * cap * 2
+    hidden = (6 + 2 + 8) * hid * n * cap * 2
     sums = 3 * n * cap * width * 2 + cap * width * 4
     return weights + rows + hidden + sums
 
@@ -374,6 +397,8 @@
             pltpu.VMEM((hid, width), bf16),
             pltpu.VMEM((rows, hid), bf16),
             pltpu.VMEM((rows, hid), bf16),
+            pltpu.VMEM((hid, 2 * rows), jnp.float32),
+            pltpu.VMEM((hid, 2 * rows), jnp.float32),
             pltpu.VMEM((cap, width), bf16),
             pltpu.VMEM((cap, width), bf16),
             dma((2,)), dma((3,)), dma((2,)),

time: 166 us -> 164 us (0.988); the launches traced: 165 us -> 161 us
  Pallas kernels: 105 us -> 98.6 us
  starting transfers between devices: 14.5 us -> 17.3 us
    pallas_call x1, Pallas kernels: 105 us -> 98.6 us  [exchange(): pl.pallas_call(functools.partial(exchange_kernel, n), out_shape=[both, bo...]
    ppermute x5, starting transfers between devices: 11.9 us -> 14.8 us  [hop(): return lax.ppermute(block, ('section', 'dp'), pairs)]
  transfers between devices with their start and end apart: 6 -> 6, of which waited for: 2 -> 2; matrix products, arithmetic and copies ran while one was open for 23% -> 23% of each run, Pallas kernels for 63% -> 61%
where the time goes in v4:
time: 164 us; the launch traced here: 161 us
  Pallas kernels  98.6 us (60%)
  matrix products  37 us (23%)
  starting transfers between devices  17.3 us (11%)
  waiting for transfers between devices  3.08 us (2%)
  other arithmetic  2.78 us (2%)
    pallas_call x1, Pallas kernels, exchange(): pl.pallas_call(functools.partial(exchange_kernel, n), out_shape=[both, bo...  98.6 us
    ppermute x5, starting transfers between devices, hop(): return lax.ppermute(block, ('section', 'dp'), pairs)  14.8 us
    dot_general x1, matrix products, per_device(): grad_up = summed(up_grad, both_acts).astype(jnp.bfloat16)[None]  11.1 us
    dot_general x1, matrix products, per_device(): grad_down = summed(hidden, both_grads).astype(jnp.bfloat16)[None]  11.1 us
    dot_general x1, matrix products, per_device(): grad_gate = summed(gate_grad, both_acts).astype(jnp.bfloat16)[None]  8.53 us
  transfers between devices with their start and end apart: 6, of which 2 were waited for; matrix products, arithmetic and copies ran while one was open for 23% of the time, Pallas kernels for 61%

profile of v4, /device:TPU:17, one launch (start us, length us, event | category | flops | bytes accessed | tf_op | source)
XLA Modules:
  0.0 160.9 jit_solution(5486583883203078680)
XLA Ops:
  0.6 0.0 copy-start
  0.6 0.9 select_reduce_fusion
  1.5 0.3 reduce-window.9
  1.9 0.1 slice.7
  2.0 0.1 slice_reduce_fusion
  2.1 0.1 fusion.19
  2.2 2.6 %collective-permute-start = (bf16[256]{0:T(256)(128)(2,1)S(1)}, bf16[256]{0:T(256)(128)(2,1)S(1)}, u32[]{:S(2)}, u32[]{:S(2)}) collective-permute-start(bf16[256]{0:T(256)(128)(2,1)S(1)} %get-tuple-element.20), channel_id=1, source_target_pairs={{4,0},{8,4},{12,8},{5,1},{9,5},{13,9},{6,2},{10,6},{14,10},{7,3},{... | collective-permute-start | bytes 1544 | tf_op jit(solution)/shard_map/ppermute | solution.py:16
  4.8 0.0 copy-done
  4.8 1.3 convolution_convert_fusion.5.acts_in
  6.0 3.0 %convolution_convert_fusion.4.grads_in = bf16[64,4096]{1,0:T(8,128)(2,1)} fusion(bf16[1,1,256,4096]{3,2,1,0:T(8,128)(2,1)} %param.8, f32[256]{0:T(256)S(1)} %get-tuple-element.22, s32[256]{0:T(256)S(1)} %get-tuple-element.21, pred[256]{0:T(512)(128)(4,1)S(1)} %reduce_or.9), kind=kOutput, calls=%fused_computation.8 | convolution fusion | flops 137658368 | bytes 2623744 | tf_op jit(solution)/shard_map/dot_general | solution.py:464
  9.0 98.6 %shard_map.102 = (bf16[2,256,4096]{2,1,0:T(8,128)(2,1)}, bf16[2,256,4096]{2,1,0:T(8,128)(2,1)}, bf16[1344,512]{1,0:T(8,128)(2,1)}, bf16[1344,512]{1,0:T(8,128)(2...) custom-call(bf16[64,4096]{1,0:T(8,128)(2,1)} %convolution_convert_fu, ...), custom_call_target="tpu_custom_call" | custom-call | flops 22548578304 | bytes 44040192 | tf_op jit(solution)/shard_map/pallas_call | solution.py:384
  107.6 1.1 dynamic-slice_bitcast_fusion
  108.7 4.6 %collective-permute-start.1 = (bf16[64,4096]{1,0:T(8,128)(2,1)S(1)}, bf16[64,4096]{1,0:T(8,128)(2,1)S(1)}, u32[]{:S(2)}, u32[]{:S(2)}) collective-permute-start(bf16[64,4096]{1,0:T(8,128)(2,1)S(1)} %dynamic-slice_bitcast_fusion), channel_id=1, source_target_pairs={{4,0},{5,1},{6,2},{7,3},{8,4},{9,5},{10,6},{11,7},{12,8},{13,9},{1... | collective-permute-start | bytes 1572872 | tf_op jit(solution)/shard_map/ppermute | solution.py:432
  113.3 1.3 collective-permute-start.2
  114.6 5.1 %collective-permute-start.4 = (bf16[64,4096]{1,0:T(8,128)(2,1)}, bf16[64,4096]{1,0:T(8,128)(2,1)}, u32[]{:S(2)}, u32[]{:S(2)}) collective-permute-start(bf16[64,4096]{1,0:T(8,128)(2,1)} %get-tuple-element.19), channel_id=1, source_target_pairs={{2,1},{3,2},{6,5},{7,6},{10,9},{11,10},{14,13},{15,14},{18,17},{19... | collective-permute-start | bytes 1572872 | tf_op jit(solution)/shard_map/ppermute | solution.py:432
  119.7 0.0 copy-start.3
  119.7 0.0 copy-start.4
  119.7 11.1 %fusion.1 = bf16[1,1344,4096]{2,1,0:T(8,128)(2,1)} fusion(bf16[1344,512]{1,0:T(8,128)(2,1)} %get-tuple-element.14, bf16[512,4096]{1,0:T(8,128)(2,1)} %bitcast.48), kind=kOutput, calls=%fused_computation.4 | convolution fusion | flops 5642649600 | bytes 16580608 | tf_op jit(solution)/shard_map/dot_general | solution.py:501
  130.8 8.5 %fusion = bf16[1,1344,4096]{2,1,0:T(8,128)(2,1)} fusion(bf16[1344,512]{1,0:T(8,128)(2,1)S(1)} %copy-done.4, bf16[512,4096]{1,0:T(8,128)(2,1)S(1)} %bitcast.49), kind=kOutput, calls=%fused_computation.3 | convolution fusion | flops 5642649600 | bytes 16580608 | tf_op jit(solution)/shard_map/dot_general | solution.py:500
  139.3 0.0 collective-permute-done.2
  139.3 0.0 collective-permute-done.4
  139.3 0.0 copy-done.2
  139.3 1.4 fusion.10
  140.8 1.9 %collective-permute-start.3 = (bf16[64,4096]{1,0:T(8,128)(2,1)S(1)}, bf16[64,4096]{1,0:T(8,128)(2,1)S(1)}, u32[]{:S(2)}, u32[]{:S(2)}) collective-permute-start(bf16[64,4096]{1,0:T(8,128)(2,1)S(1)} %get-tuple-element.24), channel_id=1, source_target_pairs={{4,1},{5,2},{6,3},{8,5},{9,6},{10,7},{12,9},{13,10},{14,11},{20,17... | collective-permute-start | bytes 1572872 | tf_op jit(solution)/shard_map/ppermute | solution.py:432
  142.7 1.9 %collective-permute-start.5 = (bf16[64,4096]{1,0:T(8,128)(2,1)S(1)}, bf16[64,4096]{1,0:T(8,128)(2,1)S(1)}, u32[]{:S(2)}, u32[]{:S(2)}) collective-permute-start(bf16[64,4096]{1,0:T(8,128)(2,1)S(1)} %get-tuple-element.25), channel_id=1, source_target_pairs={{5,0},{6,1},{7,2},{9,4},{10,5},{11,6},{13,8},{14,9},{15,10},{21,16... | collective-permute-start | bytes 1572872 | tf_op jit(solution)/shard_map/ppermute | solution.py:432
  144.6 0.0 copy-start.1
  144.6 11.1 %fusion.2 = bf16[1,1344,4096]{2,1,0:T(8,128)(2,1)} fusion(bf16[1344,512]{1,0:T(8,128)(2,1)} %get-tuple-element.15, bf16[512,4096]{1,0:T(8,128)(2,1)} %bitcast.47), kind=kOutput, calls=%fused_computation.5 | convolution fusion | flops 5642649600 | bytes 16580608 | tf_op jit(solution)/shard_map/dot_general | solution.py:502
  155.7 0.0 collective-permute-done
  155.7 0.0 collective-permute-done.1
  155.7 1.3 collective-permute-done.3
  157.0 1.8 %collective-permute-done.5 = bf16[64,4096]{1,0:T(8,128)(2,1)S(1)} collective-permute-done((bf16[64,4096]{1,0:T(8,128)(2,1)S(1)}, bf16[64,4096]{1,0:T(8,128)(2,1)S(1)}, u32[]{:S(2)}, u32[]{:S(2)}) %collective-permute-start.5) | collective-permute-done | bytes 524320 | tf_op jit(solution)/shard_map/ppermute | solution.py:432
  158.8 2.1 %fusion.3 = bf16[1,1,256,4096]{3,2,1,0:T(8,128)(2,1)} fusion(bf16[64,4096]{1,0:T(8,128)(2,1)S(1)} %collective-permute-done.5, bf16[64,4096]{1,0:T(8,128)(2,1)S(1)} %collective-permute-done.3, bf16[64,4096]{1,0:T(8,128)(2,1)S(1)} %collective-permute-done.1, s32[256]{0:T(256)S(1)} %add_convert_fusion.2), kind=kOutput, calls=%fused_computation.7 | convolution fusion | flops 136855552 | bytes 3671040 | tf_op jit(solution)/shard_map/dot_general | solution.py:26
  (8 shorter events, 0.1 us)
Async XLA Ops:
  0.6 4.1 %copy-start = (bf16[1,1,256,4096]{3,2,1,0:T(8,128)(2,1)S(1)}, bf16[1,1,256,4096]{3,2,1,0:T(8,128)(2,1)}, u32[]{:S(2)}) copy-start(bf16[1,1,256,4096]{3,2,1,0:T(8,128)(2,1)} %param.7) | copy-start | bytes 6291460
  2.2 153.5 %collective-permute-start = (bf16[256]{0:T(256)(128)(2,1)S(1)}, bf16[256]{0:T(256)(128)(2,1)S(1)}, u32[]{:S(2)}, u32[]{:S(2)}) collective-permute-start(bf16[256]{0:T(256)(128)(2,1)S(1)} %get-tuple-element.20), channel_id=1, source_target_pairs={{4,0},{8,4},{12,8},{5,1},{9,5},{13,9},{6,2},{10,6},{14,10},{7,3},{... | collective-permute-start | bytes 1544 | tf_op jit(solution)/shard_map/ppermute | solution.py:16
  108.7 47.0 %collective-permute-start.1 = (bf16[64,4096]{1,0:T(8,128)(2,1)S(1)}, bf16[64,4096]{1,0:T(8,128)(2,1)S(1)}, u32[]{:S(2)}, u32[]{:S(2)}) collective-permute-start(bf16[64,4096]{1,0:T(8,128)(2,1)S(1)} %dynamic-slice_bitcast_fusion), channel_id=1, source_target_pairs={{4,0},{5,1},{6,2},{7,3},{8,4},{9,5},{10,6},{11,7},{12,8},{13,9},{1... | collective-permute-start | bytes 1572872 | tf_op jit(solution)/shard_map/ppermute | solution.py:432
  113.3 26.0 %collective-permute-start.2 = (bf16[64,4096]{1,0:T(8,128)(2,1)}, bf16[64,4096]{1,0:T(8,128)(2,1)}, u32[]{:S(2)}, u32[]{:S(2)}) collective-permute-start(bf16[64,4096]{1,0:T(8,128)(2,1)} %get-tuple-element.18), channel_id=1, source_target_pairs={{0,1},{1,2},{4,5},{5,6},{8,9},{9,10},{12,13},{13,14},{16,17},{17,1... | collective-permute-start | bytes 1572872 | tf_op jit(solution)/shard_map/ppermute | solution.py:432
  114.6 24.7 %collective-permute-start.4 = (bf16[64,4096]{1,0:T(8,128)(2,1)}, bf16[64,4096]{1,0:T(8,128)(2,1)}, u32[]{:S(2)}, u32[]{:S(2)}) collective-permute-start(bf16[64,4096]{1,0:T(8,128)(2,1)} %get-tuple-element.19), channel_id=1, source_target_pairs={{2,1},{3,2},{6,5},{7,6},{10,9},{11,10},{14,13},{15,14},{18,17},{19... | collective-permute-start | bytes 1572872 | tf_op jit(solution)/shard_map/ppermute | solution.py:432
  119.7 11.1 %copy-start.3 = (bf16[2,256,4096]{2,1,0:T(8,128)(2,1)S(1)}, bf16[2,256,4096]{2,1,0:T(8,128)(2,1)}, u32[]{:S(2)}) copy-start(bf16[2,256,4096]{2,1,0:T(8,128)(2,1)} %get-tuple-element.13) | copy-start | bytes 12582916
  119.7 11.1 %copy-start.4 = (bf16[1344,512]{1,0:T(8,128)(2,1)S(1)}, bf16[1344,512]{1,0:T(8,128)(2,1)}, u32[]{:S(2)}) copy-start(bf16[1344,512]{1,0:T(8,128)(2,1)} %get-tuple-element.12) | copy-start | bytes 4128772
  130.8 8.5 %copy-start.2 = (bf16[256,4096]{1,0:T(8,128)(2,1)S(1)}, bf16[256,4096]{1,0:T(8,128)(2,1)}, u32[]{:S(2)}) copy-start(bf16[256,4096]{1,0:T(8,128)(2,1)} %get-tuple-element.17) | copy-start | bytes 6291460
  140.8 16.3 %collective-permute-start.3 = (bf16[64,4096]{1,0:T(8,128)(2,1)S(1)}, bf16[64,4096]{1,0:T(8,128)(2,1)S(1)}, u32[]{:S(2)}, u32[]{:S(2)}) collective-permute-start(bf16[64,4096]{1,0:T(8,128)(2,1)S(1)} %get-tuple-element.24), channel_id=1, source_target_pairs={{4,1},{5,2},{6,3},{8,5},{9,6},{10,7},{12,9},{13,10},{14,11},{20,17... | collective-permute-start | bytes 1572872 | tf_op jit(solution)/shard_map/ppermute | solution.py:432
  142.7 16.1 %collective-permute-start.5 = (bf16[64,4096]{1,0:T(8,128)(2,1)S(1)}, bf16[64,4096]{1,0:T(8,128)(2,1)S(1)}, u32[]{:S(2)}, u32[]{:S(2)}) collective-permute-start(bf16[64,4096]{1,0:T(8,128)(2,1)S(1)} %get-tuple-element.25), channel_id=1, source_target_pairs={{5,0},{6,1},{7,2},{9,4},{10,5},{11,6},{13,8},{14,9},{15,10},{21,16... | collective-permute-start | bytes 1572872 | tf_op jit(solution)/shard_map/ppermute | solution.py:432
  144.6 16.2 %copy-start.1 = (bf16[1,1,256,4096]{3,2,1,0:T(8,128)(2,1)S(1)}, bf16[1,1,256,4096]{3,2,1,0:T(8,128)(2,1)}, u32[]{:S(2)}) copy-start(bf16[1,1,256,4096]{3,2,1,0:T(8,128)(2,1)} %param.7) | copy-start | bytes 6291460
